TPU v7x, 32 devices: a whole 2x2x4 slice. The times are simulated.
32 devices in a mesh: grp: 2 (over core), blk: 16 (over z, y, x).
Axes of the slice: x: 2, y: 2, z: 4, core: 2. Of those that a mesh axis runs over, the one named last changes fastest.
Arguments:
- cell_input: bfloat16 [2, 2, 1024, 1024], P('grp', None, 'blk'), may hold values from -6 to 6
- lengths: int32 [2, 2], P('grp'), may hold values from 256 to 1024, as said below
- noise_draw: float32 [1, 2, 2, 1024, 512], P(None, 'grp', None, 'blk'), may hold values from -5 to 5
- cotangent: bfloat16 [2, 2, 1024, 1024], P('grp', None, 'blk'), may hold values from -6 to 6
- w_qkv: bfloat16 [1, 1024, 3072], P(None, None, 'blk'), may hold values from -0.1875 to 0.1875
- w_out: bfloat16 [1, 1024, 1024], P(None, None, 'blk'), may hold values from -1 to 1
- w_ffn_in: bfloat16 [1, 1024, 4096], P(None, None, 'blk'), may hold values from -0.1875 to 0.1875
- w_ffn_out: bfloat16 [1, 4096, 1024], P(None, None, 'blk'), may hold values from -0.09375 to 0.09375
- w_latent: bfloat16 [1, 1024, 1024], P(None, None, 'blk'), may hold values from -0.0625 to 0.0625
- w_decode: bfloat16 [1, 512, 1024], P(None, None, 'blk'), may hold values from -0.125 to 0.125
- vectors: bfloat16 [1, 9, 1024], P(None, None, 'blk')
- inner_bias: bfloat16 [1, 5120], P(None, 'blk'), may hold values from -3 to 3
- prior_means: bfloat16 [1, 16, 512], P(None, None, 'blk'), may hold values from -3 to 3
- prior_logvars: bfloat16 [1, 16, 512], P(None, None, 'blk'), may hold values from 2 to 3
Outputs:
- layer_out: float32 [2, 2, 1024, 1024], P('grp', None, 'blk')
- grad_cells: float32 [2, 2, 1024, 1024], P('grp', None, 'blk')
- kl_mean: float32 [], replicated
- grad_qkv: float32 [1, 1024, 3072], P(None, None, 'blk')
- grad_out: float32 [1, 1024, 1024], P(None, None, 'blk')
- grad_ffn_in: float32 [1, 1024, 4096], P(None, None, 'blk')
- grad_ffn_out: float32 [1, 4096, 1024], P(None, None, 'blk')
- grad_latent: float32 [1, 1024, 1024], P(None, None, 'blk')
- grad_decode: float32 [1, 512, 1024], P(None, None, 'blk')
- grad_vectors: float32 [1, 9, 1024], P(None, None, 'blk')
- grad_inner: float32 [1, 5120], P(None, 'blk')
- grad_means: float32 [1, 16, 512], P(None, None, 'blk')
- grad_logvars: float32 [1, 16, 512], P(None, None, 'blk')
Inputs may be any that keep to these rules, and one draw needn't show every extreme that they name: In every group one slide has exactly 1024 cells; a slide's cells are the first lengths of its slot.
All inputs are finite; a program needn't handle non-finite values.
Results may differ from a plain program's by a relative error of at most 0.0085.
Values may be sent and summed in bfloat16 or wider, within the bound.
No kernel may reach another device: no remote copies, remote signals or barrier semaphores. Data moves between devices by JAX's collectives and lax.ppermute only.
A program may use at most 256 MiB of HBM per device.

v0:
```python
import math

import jax
import jax.numpy as jnp
from jax import lax
from jax.sharding import PartitionSpec as P

HEADS = 16
LAYERS = 1
HEAD_DIM = 64


EPS_NORM = 1e-05
MASKED = -1e30


def to_low(values):
    return values.astype(jnp.bfloat16)


def product(left, right):
    return jnp.dot(left, right, preferred_element_type=jnp.float32)


def product_tn(left, right):
    return lax.dot_general(
        left, right, (((0,), (0,)), ((), ())), preferred_element_type=jnp.float32
    )


def product_nt(left, right):
    return lax.dot_general(
        left, right, (((1,), (1,)), ((), ())), preferred_element_type=jnp.float32
    )


def layer_norm(values, norm_gain, norm_shift):
    centre = values - jnp.mean(values, axis=-1, keepdims=True)
    spread = jnp.mean(centre * centre, axis=-1, keepdims=True)
    return centre * lax.rsqrt(spread + EPS_NORM) * norm_gain + norm_shift


def mixture_kl(sample, noise_rows, logvar, mean_rows, logvars):
    own_term = jnp.sum(-0.5 * noise_rows * noise_rows - 0.5 * logvar, axis=-1)
    offset = sample[:, None, :] - mean_rows[None, :, :]
    component = jnp.sum(
        -0.5 * offset * offset * jnp.exp(-logvars)[None] - 0.5 * logvars[None], axis=-1
    ) - math.log(mean_rows.shape[0])
    row_peak = jnp.max(component, axis=-1, keepdims=True)
    mixture = row_peak[:, 0] + jnp.log(jnp.sum(jnp.exp(component - row_peak), axis=-1))
    return own_term - mixture


def bottleneck(latent, noise_rows, live_rows, mean_rows, logvars):
    lat_width = noise_rows.shape[-1]
    mean_part = latent[:, :lat_width]
    logvar = latent[:, lat_width:]
    sample = mean_part + jnp.exp(0.5 * logvar) * noise_rows
    per_cell = mixture_kl(sample, noise_rows, logvar, mean_rows, logvars)
    return (sample, jnp.sum(jnp.where(live_rows, per_cell, 0.0)) / lat_width)


def slot_scores(query_slots, keys_all, slide_len, score_scale):
    slot_count, query_rows, model_width = query_slots.shape
    heads_q = query_slots.reshape(slot_count, query_rows, HEADS, HEAD_DIM)
    heads_k = keys_all.reshape(slot_count, keys_all.shape[1], HEADS, HEAD_DIM)
    raw_scores = (
        jnp.einsum("sqhd,skhd->shqk", heads_q, heads_k, preferred_element_type=jnp.float32)
        * score_scale
    )
    live_keys = jnp.arange(keys_all.shape[1])[None, :] < slide_len[:, None]
    return jnp.where(live_keys[:, None, None, :], raw_scores, MASKED)


def widen(gathered):
    qkv_w, out_w, in_w, back_w, latent_w, decode_w, vec_rows, inner_rows, mean_rows, logvars = (
        gathered
    )
    return (
        qkv_w,
        out_w,
        in_w,
        back_w,
        latent_w,
        decode_w,
        vec_rows.astype(jnp.float32),
        inner_rows.astype(jnp.float32),
        mean_rows.astype(jnp.float32),
        logvars.astype(jnp.float32),
    )


def gather_weights(layer_parts):
    (
        part_qkv,
        part_out,
        part_in,
        part_back,
        part_latent,
        part_decode,
        part_vectors,
        part_inner,
        part_means,
        part_logvars,
    ) = layer_parts
    return widen(
        (
            lax.all_gather(part_qkv, "blk", axis=1, tiled=True),
            lax.all_gather(part_out, "blk", axis=1, tiled=True),
            lax.all_gather(part_in, "blk", axis=1, tiled=True),
            lax.all_gather(part_back, "blk", axis=1, tiled=True),
            lax.all_gather(part_latent, "blk", axis=1, tiled=True),
            lax.all_gather(part_decode, "blk", axis=1, tiled=True),
            lax.all_gather(part_vectors, "blk", axis=1, tiled=True),
            lax.all_gather(part_inner, "blk", axis=0, tiled=True),
            lax.all_gather(part_means, "blk", axis=1, tiled=True),
            lax.all_gather(part_logvars, "blk", axis=1, tiled=True),
        )
    )


def reduce_grads(grads):
    (
        grad_qkv_w,
        grad_out_w,
        grad_in_w,
        grad_back_w,
        grad_latent_w,
        grad_decode_w,
        grad_vec,
        grad_inner,
        grad_mean_rows,
        grad_logvars,
    ) = grads
    (
        shard_qkv,
        shard_out,
        shard_in,
        shard_back,
        shard_latent,
        shard_decode,
        shard_vec,
        shard_inner,
        shard_means,
        shard_logvars,
    ) = (
        lax.psum_scatter(grad_qkv_w, "blk", scatter_dimension=1, tiled=True),
        lax.psum_scatter(grad_out_w, "blk", scatter_dimension=1, tiled=True),
        lax.psum_scatter(grad_in_w, "blk", scatter_dimension=1, tiled=True),
        lax.psum_scatter(grad_back_w, "blk", scatter_dimension=1, tiled=True),
        lax.psum_scatter(grad_latent_w, "blk", scatter_dimension=1, tiled=True),
        lax.psum_scatter(grad_decode_w, "blk", scatter_dimension=1, tiled=True),
        lax.psum_scatter(grad_vec, "blk", scatter_dimension=1, tiled=True),
        lax.psum_scatter(grad_inner, "blk", scatter_dimension=0, tiled=True),
        lax.psum_scatter(grad_mean_rows, "blk", scatter_dimension=1, tiled=True),
        lax.psum_scatter(grad_logvars, "blk", scatter_dimension=1, tiled=True),
    )
    return lax.psum(
        (
            shard_qkv,
            shard_out,
            shard_in,
            shard_back,
            shard_latent,
            shard_decode,
            shard_vec,
            shard_inner,
            shard_means,
            shard_logvars,
        ),
        "grp",
    )


def layer_forward(hidden, full_weights, noise_rows, live_rows, slide_len, score_scale):
    qkv_w, out_w, in_w, back_w, latent_w, decode_w, vec_rows, inner_rows, mean_rows, logvars = (
        full_weights
    )
    model_width = hidden.shape[1]
    slot_count = slide_len.shape[0]
    slot_span = hidden.shape[0] // slot_count
    ff_width = in_w.shape[1]
    normed = to_low(layer_norm(hidden, vec_rows[0], vec_rows[1]))
    qkv_all = product(normed, qkv_w)
    query_low = to_low(qkv_all[:, :model_width] + vec_rows[2])
    keys_own = to_low(qkv_all[:, model_width : 2 * model_width])
    values_own = to_low(qkv_all[:, 2 * model_width :] + vec_rows[3])
    keys_all, values_all = (
        lax.all_gather(
            keys_own.reshape(slot_count, slot_span, model_width), "blk", axis=1, tiled=True
        ),
        lax.all_gather(
            values_own.reshape(slot_count, slot_span, model_width), "blk", axis=1, tiled=True
        ),
    )
    scores = slot_scores(
        query_low.reshape(slot_count, slot_span, model_width), keys_all, slide_len, score_scale
    )
    row_peak = jnp.max(scores, axis=-1, keepdims=True)
    weights = jnp.exp(scores - row_peak)
    totals = jnp.sum(weights, axis=-1, keepdims=True)
    probs_low = to_low(weights / totals)
    log_total = row_peak + jnp.log(totals)
    heads_v = values_all.reshape(slot_count, values_all.shape[1], HEADS, HEAD_DIM)
    mixed_f = jnp.einsum("shqk,skhd->sqhd", probs_low, heads_v, preferred_element_type=jnp.float32)
    mixed_low = to_low(mixed_f.reshape(slot_count * slot_span, model_width))
    attended = hidden + product(mixed_low, out_w) + vec_rows[4]
    normed_two = to_low(layer_norm(attended, vec_rows[5], vec_rows[6]))
    inner_act = product(normed_two, in_w) + inner_rows[:ff_width]
    activated = to_low(jax.nn.gelu(inner_act))
    fed_rows = attended + product(activated, back_w) + vec_rows[7]
    fed_low = to_low(fed_rows)
    latent = product(fed_low, latent_w) + inner_rows[ff_width:]
    sample, kl_part = bottleneck(latent, noise_rows, live_rows, mean_rows, logvars)
    sample_low = to_low(sample)
    output = fed_rows + product(sample_low, decode_w) + vec_rows[8]
    saved_state = (
        hidden,
        normed,
        query_low,
        keys_own,
        values_own,
        log_total,
        mixed_low,
        attended,
        normed_two,
        inner_act,
        activated,
        fed_low,
        latent,
        sample_low,
    )
    return (output, kl_part, saved_state)


def layer_backward(
    grad_out, full_weights, saved_state, noise_rows, live_rows, slide_len, score_scale
):
    qkv_w, out_w, in_w, back_w, latent_w, decode_w, vec_rows, inner_rows, mean_rows, logvars = (
        full_weights
    )
    (
        hidden,
        normed,
        query_low,
        keys_own,
        values_own,
        log_total,
        mixed_low,
        attended,
        normed_two,
        inner_act,
        activated,
        fed_low,
        latent,
        sample_low,
    ) = saved_state
    model_width = hidden.shape[1]
    row_total = hidden.shape[0]
    slot_count = slide_len.shape[0]
    slot_span = row_total // slot_count
    grad_dec_low = to_low(grad_out)
    grad_decode_w = product_tn(sample_low, grad_dec_low)
    grad_sample = product_nt(grad_dec_low, decode_w)

    def bottle(latent_in, means_in, logvars_in):
        return bottleneck(latent_in, noise_rows, live_rows, means_in, logvars_in)

    ignored, bottle_pull = jax.vjp(bottle, latent, mean_rows, logvars)
    grad_latent_f, grad_mean_rows, grad_logvars = bottle_pull(
        (grad_sample, jnp.ones((), jnp.float32))
    )
    grad_latent_low = to_low(grad_latent_f)
    grad_latent_w = product_tn(fed_low, grad_latent_low)
    grad_fed = grad_out + product_nt(grad_latent_low, latent_w)
    grad_fed_low = to_low(grad_fed)
    grad_back_w = product_tn(activated, grad_fed_low)
    grad_act = product_nt(grad_fed_low, back_w)
    ignored_two, gelu_pull = jax.vjp(jax.nn.gelu, inner_act)
    grad_inner_low = to_low(gelu_pull(grad_act)[0])
    grad_in_w = product_tn(normed_two, grad_inner_low)
    grad_normed_two = product_nt(grad_inner_low, in_w)
    ignored_three, second_pull = jax.vjp(layer_norm, attended, vec_rows[5], vec_rows[6])
    grad_att_norm, grad_gain_two, grad_shift_two = second_pull(grad_normed_two)
    grad_attended = grad_fed + grad_att_norm
    grad_proj_low = to_low(grad_attended)
    grad_out_w = product_tn(mixed_low, grad_proj_low)
    grad_mixed_low = to_low(product_nt(grad_proj_low, out_w))
    keys_all, values_all = (
        lax.all_gather(
            keys_own.reshape(slot_count, slot_span, model_width), "blk", axis=1, tiled=True
        ),
        lax.all_gather(
            values_own.reshape(slot_count, slot_span, model_width), "blk", axis=1, tiled=True
        ),
    )
    grad_mixed_heads = grad_mixed_low.reshape(slot_count, slot_span, HEADS, HEAD_DIM)
    heads_k = keys_all.reshape(slot_count, keys_all.shape[1], HEADS, HEAD_DIM)
    heads_v = values_all.reshape(slot_count, values_all.shape[1], HEADS, HEAD_DIM)
    scores = slot_scores(
        query_low.reshape(slot_count, slot_span, model_width), keys_all, slide_len, score_scale
    )
    probs_f = jnp.exp(scores - log_total)
    grad_probs = jnp.einsum(
        "sqhd,skhd->shqk", grad_mixed_heads, heads_v, preferred_element_type=jnp.float32
    )
    centre = jnp.sum(grad_probs * probs_f, axis=-1, keepdims=True)
    grad_scores_low = to_low(probs_f * (grad_probs - centre))
    grad_query = (
        jnp.einsum("shqk,skhd->sqhd", grad_scores_low, heads_k, preferred_element_type=jnp.float32)
        * score_scale
    )
    grad_query_low = to_low(grad_query.reshape(row_total, model_width))
    rows_all, mixed_all = (
        lax.all_gather(
            query_low.reshape(slot_count, slot_span, model_width), "blk", axis=1, tiled=True
        ),
        lax.all_gather(
            grad_mixed_low.reshape(slot_count, slot_span, model_width), "blk", axis=1, tiled=True
        ),
    )
    total_all, centre_all = (
        lax.all_gather(log_total, "blk", axis=2, tiled=True),
        lax.all_gather(centre, "blk", axis=2, tiled=True),
    )
    query_all = rows_all.reshape(slot_count, rows_all.shape[1], HEADS, HEAD_DIM)
    dmixed_all = mixed_all.reshape(slot_count, mixed_all.shape[1], HEADS, HEAD_DIM)
    own_keys = keys_own.reshape(slot_count, slot_span, HEADS, HEAD_DIM)
    own_values = values_own.reshape(slot_count, slot_span, HEADS, HEAD_DIM)
    own_raw = (
        jnp.einsum("sqhd,skhd->shqk", query_all, own_keys, preferred_element_type=jnp.float32)
        * score_scale
    )
    key_places = lax.axis_index("blk") * slot_span + jnp.arange(slot_span)
    live_own = key_places[None, :] < slide_len[:, None]
    own_scores = jnp.where(live_own[:, None, None, :], own_raw, MASKED)
    own_probs = jnp.exp(own_scores - total_all)
    own_dprobs = jnp.einsum(
        "sqhd,skhd->shqk", dmixed_all, own_values, preferred_element_type=jnp.float32
    )
    own_dscores = to_low(own_probs * (own_dprobs - centre_all))
    grad_keys = (
        jnp.einsum("shqk,sqhd->skhd", own_dscores, query_all, preferred_element_type=jnp.float32)
        * score_scale
    )
    grad_values = jnp.einsum(
        "shqk,sqhd->skhd", to_low(own_probs), dmixed_all, preferred_element_type=jnp.float32
    )
    grad_keys_low = to_low(grad_keys.reshape(row_total, model_width))
    grad_values_low = to_low(grad_values.reshape(row_total, model_width))
    grad_qkv_low = jnp.concatenate([grad_query_low, grad_keys_low, grad_values_low], axis=1)
    grad_qkv_w = product_tn(normed, grad_qkv_low)
    grad_normed = product_nt(grad_qkv_low, qkv_w)
    ignored_four, first_pull = jax.vjp(layer_norm, hidden, vec_rows[0], vec_rows[1])
    grad_hid_norm, grad_gain_one, grad_shift_one = first_pull(grad_normed)
    grad_hidden = grad_attended + grad_hid_norm
    grad_vec = jnp.stack(
        [
            grad_gain_one,
            grad_shift_one,
            jnp.sum(grad_query_low.astype(jnp.float32), axis=0),
            jnp.sum(grad_values_low.astype(jnp.float32), axis=0),
            jnp.sum(grad_attended, axis=0),
            grad_gain_two,
            grad_shift_two,
            jnp.sum(grad_fed, axis=0),
            jnp.sum(grad_out, axis=0),
        ]
    )
    grad_inner = jnp.concatenate(
        [
            jnp.sum(grad_inner_low.astype(jnp.float32), axis=0),
            jnp.sum(grad_latent_low.astype(jnp.float32), axis=0),
        ]
    )
    return (
        grad_hidden,
        (
            grad_qkv_w,
            grad_out_w,
            grad_in_w,
            grad_back_w,
            grad_latent_w,
            grad_decode_w,
            grad_vec,
            grad_inner,
            grad_mean_rows,
            grad_logvars,
        ),
    )


def per_device(
    cell_input,
    lengths,
    noise_draw,
    cotangent,
    w_qkv,
    w_out,
    w_ffn_in,
    w_ffn_out,
    w_latent,
    w_decode,
    vectors,
    inner_bias,
    prior_means,
    prior_logvars,
):
    slot_count = cell_input.shape[1]
    slot_span = cell_input.shape[2]
    model_width = cell_input.shape[3]
    row_total = slot_count * slot_span
    lat_width = noise_draw.shape[-1]
    cycle_size = lax.axis_size("blk")
    score_scale = 1.0 / math.sqrt(HEAD_DIM)
    slide_len = lengths[0]
    positions = lax.axis_index("blk") * slot_span + jnp.arange(slot_span)
    live_rows = (positions[None, :] < slide_len[:, None]).reshape(row_total)
    hidden = cell_input[0].reshape(row_total, model_width).astype(jnp.float32)
    stacks = (
        w_qkv,
        w_out,
        w_ffn_in,
        w_ffn_out,
        w_latent,
        w_decode,
        vectors,
        inner_bias,
        prior_means,
        prior_logvars,
    )
    layer_idx = 0
    full_weights = gather_weights([stacked[layer_idx] for stacked in stacks])
    kept_weights = [full_weights]
    hidden, kl_part, saved_state = layer_forward(
        hidden,
        full_weights,
        noise_draw[layer_idx, 0].reshape(row_total, lat_width),
        live_rows,
        slide_len,
        score_scale,
    )
    saved_layers = [saved_state]
    layer_out = hidden.reshape(1, slot_count, slot_span, model_width)
    kl_total = lax.psum(kl_part, ("grp", "blk"))
    kl_mean = kl_total / (lax.axis_size("grp") * cycle_size * row_total)
    grad_rows = cotangent[0].reshape(row_total, model_width).astype(jnp.float32)
    reduced = [None] * LAYERS
    for layer_idx in reversed(range(LAYERS)):
        full_weights = kept_weights[layer_idx]
        grad_rows, grads = layer_backward(
            grad_rows,
            full_weights,
            saved_layers[layer_idx],
            noise_draw[layer_idx, 0].reshape(row_total, lat_width),
            live_rows,
            slide_len,
            score_scale,
        )
        reduced[layer_idx] = reduce_grads(grads)
    grad_cells = grad_rows.reshape(1, slot_count, slot_span, model_width)
    stacked_grads = [jnp.stack([reduced[0][member]]) for member in range(10)]
    return (
        layer_out,
        grad_cells,
        kl_mean,
        stacked_grads[0],
        stacked_grads[1],
        stacked_grads[2],
        stacked_grads[3],
        stacked_grads[4],
        stacked_grads[5],
        stacked_grads[6],
        stacked_grads[7],
        stacked_grads[8],
        stacked_grads[9],
    )


def solution(mesh):
    placed = (
        P("grp", None, "blk", None),
        P("grp", None),
        P(None, "grp", None, "blk", None),
        P("grp", None, "blk", None),
        P(None, None, "blk"),
        P(None, None, "blk"),
        P(None, None, "blk"),
        P(None, None, "blk"),
        P(None, None, "blk"),
        P(None, None, "blk"),
        P(None, None, "blk"),
        P(None, "blk"),
        P(None, None, "blk"),
        P(None, None, "blk"),
    )
    return jax.shard_map(
        per_device,
        mesh=mesh,
        in_specs=placed,
        out_specs=(
            P("grp", None, "blk", None),
            P("grp", None, "blk", None),
            P(),
            P(None, None, "blk"),
            P(None, None, "blk"),
            P(None, None, "blk"),
            P(None, None, "blk"),
            P(None, None, "blk"),
            P(None, None, "blk"),
            P(None, None, "blk"),
            P(None, "blk"),
            P(None, None, "blk"),
            P(None, None, "blk"),
        ),
        check_vma=False,
    )
```

profile of v0, /device:TPU:0, one launch (start us, length us, event | category | flops | bytes accessed | tf_op | source)
XLA Modules:
  0.0 2337.5 jit_solution(862927641251473955)
XLA Ops:
  8.8 47.5 %all-gather = bf16[1,9,1024]{1,0,2:T(2,128)(2,1)S(1)} all-gather(bf16[1,9,64]{1,0,2:T(2,128)(2,1)S(1)} %copy.154), channel_id=2, replica_groups=mesh['grp'=2,'blk'=16] {'blk'}, dimensions={2}, use_global_device_ids=true | all-gather | bytes 19584 | tf_op jit(solution)/shard_map/all_gather | solution.py:114
  59.3 31.0 %slice_reduce_fusion = (f32[1024]{0:T(1024)}, f32[1024]{0:T(1024)}, f32[1024]{0:T(1024)S(1)}, f32[1024]{0:T(1024)S(1)}, f32[1024]{0:T(1024)S(1)}, /*index=5*/f32...) fusion(f32[1,9,1024]{1,0,2:T(1,128)S(1)} %convert_element_type.180), kind=kLoop, calls=%fused_computation.91 | loop fusion | bytes 73728 | tf_op jit(solution)/shard_map/slice | solution.py:216
  90.6 19.1 all-gather.31.cloned.1.call-done
  109.7 5.0 fusion.12
  121.6 75.0 %all-reduce.2 = bf16[5120]{0:T(1024)(128)(2,1)S(1)} all-reduce(bf16[5120]{0:T(1024)(128)(2,1)S(1)} %dynamic-update-slice), channel_id=6, replica_groups=mesh['grp'=2,'blk'=16] {'blk'}, use_global_device_ids=true, to_apply=%add.2 | all-reduce | flops 5120 | bytes 20480
  197.4 37.5 %all-gather.9 = bf16[1,16,512]{1,0,2:T(2,128)(2,1)S(1)} all-gather(bf16[1,16,32]{1,0,2:T(2,128)(2,1)S(1)} %copy.161), channel_id=11, replica_groups=mesh['grp'=2,'blk'=16] {'blk'}, dimensions={2}, use_global_device_ids=true | all-gather | bytes 17408 | tf_op jit(solution)/shard_map/all_gather | solution.py:117
  235.1 40.6 %all-gather.8 = bf16[1,16,512]{1,0,2:T(2,128)(2,1)S(1)} all-gather(bf16[1,16,32]{1,0,2:T(2,128)(2,1)S(1)} %copy.159), channel_id=10, replica_groups=mesh['grp'=2,'blk'=16] {'blk'}, dimensions={2}, use_global_device_ids=true | all-gather | bytes 17408 | tf_op jit(solution)/shard_map/all_gather | solution.py:116
  277.2 6.3 copy.156
  283.5 3.8 fusion.19
  287.3 3.2 copy-done
  292.5 6.2 copy.155
  298.8 7.4 fusion.78
  307.0 28.2 %all-gather.33.cloned.1.call-done = bf16[1,1024,1024]{1,2,0:T(8,128)(2,1)} async-done(((bf16[1,1024,64]{1,2,0:T(8,128)(2,1)}), bf16[1,1024,1024]{1,2,0:T(8,128)(2,1)}) %all-gather.33.cloned.1.call-update) | async-done | bytes 2097168 | tf_op jit(solution)/shard_map/all_gather | solution.py:109
  335.2 2.5 fusion.139
  338.0 133.7 %all-gather.35.cloned.1.call-done = bf16[1,1024,4096]{2,1,0:T(8,128)(2,1)} async-done(((bf16[1,1024,256]{2,1,0:T(8,128)(2,1)}), bf16[1,1024,4096]{2,1,0:T(8,128)(2,1)}) %all-gather.35.cloned.1.call-update) | async-done | bytes 8388624 | tf_op jit(solution)/shard_map/all_gather | solution.py:110
  471.8 4.7 fusion.16
  476.5 108.9 %all-gather.37.cloned.1.call-done = bf16[1,4096,1024]{1,2,0:T(8,128)(2,1)} async-done(((bf16[1,4096,64]{1,2,0:T(8,128)(2,1)}), bf16[1,4096,1024]{1,2,0:T(8,128)(2,1)}) %all-gather.37.cloned.1.call-update) | async-done | bytes 8388624 | tf_op jit(solution)/shard_map/all_gather | solution.py:111
  585.4 6.3 fusion.83
  591.7 55.4 %all-gather.39.cloned.1.call-done = bf16[1,1024,1024]{1,2,0:T(8,128)(2,1)} async-done(((bf16[1,1024,64]{1,2,0:T(8,128)(2,1)}), bf16[1,1024,1024]{1,2,0:T(8,128)(2,1)}) %all-gather.39.cloned.1.call-update) | async-done | bytes 2097168 | tf_op jit(solution)/shard_map/all_gather | solution.py:112
  647.1 2.4 fusion.72
  657.6 2.0 fusion.135
  660.5 4.0 fusion.36
  664.5 39.4 %all-gather.41.cloned.1.call-done = bf16[1,512,1024]{1,2,0:T(8,128)(2,1)} async-done(((bf16[1,512,64]{1,2,0:T(8,128)(2,1)}), bf16[1,512,1024]{1,2,0:T(8,128)(2,1)}) %all-gather.41.cloned.1.call-update) | async-done | bytes 1048592 | tf_op jit(solution)/shard_map/all_gather | solution.py:113
  703.8 2.4 fusion.102
  707.0 2.2 fusion.75
  709.3 7.0 convert_reduce_fusion
  716.3 3.6 multiply_reduce_fusion.1
  722.1 2.8 fusion.115
  725.0 3.7 fusion.106
  728.8 3.9 fusion.112
  732.8 2.1 reshape.301
  734.9 2.1 reshape.304
  737.0 2.1 reshape.298
  739.3 10.8 multiply_reduce_fusion
  750.7 10.1 convert_reduce_fusion.2
  762.0 2.1 convert_element_type.165
  764.1 49.7 %all-gather.11 = f32[2,16,1024]{1,0,2:T(2,128)} all-gather(f32[2,16,64]{1,0,2:T(2,128)} %copy.173), channel_id=13, replica_groups=mesh['grp'=2,'blk'=16] {'blk'}, dimensions={2}, use_global_device_ids=true | all-gather | bytes 139264 | tf_op jit(solution)/shard_map/all_gather | solution.py:324
  813.8 2.0 copy.174
  815.8 53.2 %all-gather.10 = f32[2,16,1024]{1,0,2:T(2,128)} all-gather(f32[2,16,64]{1,0,2:T(2,128)S(1)} %copy.169), channel_id=12, replica_groups=mesh['grp'=2,'blk'=16] {'blk'}, dimensions={2}, use_global_device_ids=true | all-gather | bytes 139264 | tf_op jit(solution)/shard_map/all_gather | solution.py:323
  870.4 6.2 copy.167
  878.3 6.8 fusion.95
  885.1 6.3 copy.171
  891.4 10.6 fusion.79
  902.0 2.2 copy.176
  904.2 2.1 convert_element_type.169
  906.3 7.3 convert_reduce_fusion.1
  914.7 2.1 convert_element_type.173
  920.2 7.5 fusion.140
  928.4 9.4 fusion.133
  938.9 8.1 fusion.109
  950.1 3.9 fusion.134
  958.3 94.6 %reduce-scatter.18.cloned.1.call-done = f32[1024,64]{0,1:T(8,128)} async-done(((f32[1024,1024]{0,1:T(8,128)}), f32[1024,64]{0,1:T(8,128)}) %reduce-scatter.18.cloned.1.call-update) | async-done | bytes 262160 | tf_op jit(solution)/shard_map/reduce_scatter | solution.py:148
  1052.9 97.0 %reduce-scatter.24.cloned.1.call-done = f32[1024,64]{0,1:T(8,128)} async-done(((f32[1024,1024]{0,1:T(8,128)}), f32[1024,64]{0,1:T(8,128)}) %reduce-scatter.24.cloned.1.call-update) | async-done | bytes 262160 | tf_op jit(solution)/shard_map/reduce_scatter | solution.py:151
  1149.9 209.2 %reduce-scatter.16.cloned.1.call-done = f32[1024,192]{0,1:T(8,128)} async-done(((f32[1024,3072]{0,1:T(8,128)}), f32[1024,192]{0,1:T(8,128)}) %reduce-scatter.16.cloned.1.call-update) | async-done | bytes 786448 | tf_op jit(solution)/shard_map/reduce_scatter | solution.py:147
  1359.1 348.3 %reduce-scatter.20.cloned.1.call-done = f32[1024,256]{1,0:T(8,128)} async-done(((f32[1024,4096]{1,0:T(8,128)}), f32[1024,256]{1,0:T(8,128)}) %reduce-scatter.20.cloned.1.call-update) | async-done | bytes 1048592 | tf_op jit(solution)/shard_map/reduce_scatter | solution.py:149
  1707.4 354.3 %reduce-scatter.22.cloned.1.call-done = f32[4096,64]{0,1:T(8,128)} async-done(((f32[4096,1024]{0,1:T(8,128)}), f32[4096,64]{0,1:T(8,128)}) %reduce-scatter.22.cloned.1.call-update) | async-done | bytes 1048592 | tf_op jit(solution)/shard_map/reduce_scatter | solution.py:150
  2064.3 44.5 %psum.77 = f32[]{:T(128)} all-reduce(f32[]{:T(128)S(6)} %div.77), channel_id=1, replica_groups=mesh['grp'=2,'blk'=16] {'grp','blk'}, use_global_device_ids=true, to_apply=%region_19.20 | all-reduce | flops 1 | bytes 8 | tf_op jit(solution)/shard_map/psum | solution.py:445
  2109.8 77.2 %all-reduce.3 = f32[5120]{0:T(1024)S(1)} all-reduce(f32[5120]{0:T(1024)S(1)} %pad_maximum_fusion), channel_id=21, replica_groups=mesh['grp'=2,'blk'=16] {'blk'}, use_global_device_ids=true, to_apply=%region_45.46.clone | all-reduce | flops 5120 | bytes 40960
  2189.8 31.7 %reduce-scatter.32.cloned.1.call-done = f32[32,16]{1,0:T(8,128)} async-done(((f32[512,16]{1,0:T(8,128)}), f32[32,16]{1,0:T(8,128)}) %reduce-scatter.32.cloned.1.call-update) | async-done | bytes 2064
  2224.0 73.4 %reduce-scatter.28.cloned.1.call-done = f32[64,9]{1,0:T(8,128)} async-done(((f32[1024,9]{1,0:T(8,128)}), f32[64,9]{1,0:T(8,128)}) %reduce-scatter.28.cloned.1.call-update) | async-done | bytes 2320
  2298.2 4.0 all-reduce.4
  2302.8 17.9 all-reduce.8.cloned.1.call-done
  2320.6 2.2 copy.208
  2324.5 2.3 copy.210
  (277 shorter events, 58.9 us)
Async XLA Ops:
  7.2 83.1 %copy-start.1 = (bf16[1,2,64,1024]{3,2,1,0:T(8,128)(2,1)S(1)}, bf16[1,2,64,1024]{3,2,1,0:T(8,128)(2,1)}, u32[]{:S(2)}) copy-start(bf16[1,2,64,1024]{3,2,1,0:T(8,128)(2,1)} %param.14) | copy-start | bytes 786436
  7.2 102.5 %all-gather.31.cloned.1.call-start = ((), (), s32[]{:S(2)}) async-start(), calls=%async_computation.19 | async-start | bytes 6684672 | tf_op jit(solution)/shard_map/all_gather | solution.py:108
  7.9 269.3 %all-gather.25.cloned.1.call-start = ((), (), s32[]{:S(2)}) async-start(), calls=%async_computation.10 | async-start | bytes 4456448 | tf_op jit(solution)/shard_map/all_gather | solution.py:189
  58.0 56.7 %copy-start.48 = (f32[128]{0:T(128)}, f32[128]{0:T(128)S(1)}, u32[]{:S(2)}) copy-start(f32[128]{0:T(128)S(1)} %div.63) | copy-start | bytes 1540
  59.3 31.3 %copy-start.66 = (f32[128]{0:T(128)}, f32[128]{0:T(128)S(1)}, u32[]{:S(2)}) copy-start(f32[128]{0:T(128)S(1)} %add.225) | copy-start | bytes 1540
  59.3 55.4 %copy-start.52 = (f32[128]{0:T(128)}, f32[128]{0:T(128)S(1)}, u32[]{:S(2)}) copy-start(f32[128]{0:T(128)S(1)} %rsqrt.22) | copy-start | bytes 1540
  90.5 24.9 %copy-start.17 = (bf16[128,1024]{1,0:T(8,128)(2,1)}, bf16[128,1024]{1,0:T(8,128)(2,1)S(1)}, u32[]{:S(2)}) copy-start(bf16[128,1024]{1,0:T(8,128)(2,1)S(1)} %add_convert_fusion.2) | copy-start | bytes 786436
  90.6 29.5 %copy-start.60 = (bf16[1,320]{1,0:T(2,128)(2,1)S(1)}, bf16[1,320]{1,0:T(2,128)(2,1)}, u32[]{:S(2)}) copy-start(bf16[1,320]{1,0:T(2,128)(2,1)} %param.25) | copy-start | bytes 1924
  90.6 29.5 %copy-start.59 = (u32[32]{0:T(128)S(1)}, u32[32]{0:T(128)}, u32[]{:S(2)}) copy-start(u32[32]{0:T(128)} %constant.69) | copy-start | bytes 388
  90.6 106.0 %copy-start.62 = (s32[1,2]{1,0:T(1,128)S(1)}, s32[1,2]{1,0:T(1,128)}, u32[]{:S(2)}) copy-start(s32[1,2]{1,0:T(1,128)} %param.15) | copy-start | bytes 28
  90.6 106.7 %copy-start.54 = (bf16[1,16,32]{2,1,0:T(8,128)(2,1)S(1)}, bf16[1,16,32]{2,1,0:T(8,128)(2,1)}, u32[]{:S(2)}) copy-start(bf16[1,16,32]{2,1,0:T(8,128)(2,1)} %param.27) | copy-start | bytes 3076
  114.7 120.3 %copy-start.55 = (bf16[1,16,32]{2,1,0:T(8,128)(2,1)S(1)}, bf16[1,16,32]{2,1,0:T(8,128)(2,1)}, u32[]{:S(2)}) copy-start(bf16[1,16,32]{2,1,0:T(8,128)(2,1)} %param.26) | copy-start | bytes 3076
  115.5 177.1 %all-gather.23.cloned.1.call-start = ((), (), s32[]{:S(2)}) async-start(), calls=%async_computation.9 | async-start | bytes 4456448 | tf_op jit(solution)/shard_map/all_gather | solution.py:192
  116.3 160.8 %copy-start.18 = (bf16[128,1024]{1,0:T(8,128)(2,1)}, bf16[128,1024]{1,0:T(8,128)(2,1)S(1)}, u32[]{:S(2)}) copy-start(bf16[128,1024]{1,0:T(8,128)(2,1)S(1)} %get-tuple-element.115) | copy-start | bytes 786436
  116.4 218.9 %all-gather.33.cloned.1.call-start = ((), (), s32[]{:S(2)}) async-start(), calls=%async_computation.20 | async-start | bytes 2228224 | tf_op jit(solution)/shard_map/all_gather | solution.py:109
  117.0 354.8 %all-gather.35.cloned.1.call-start = ((), (), s32[]{:S(2)}) async-start(), calls=%async_computation.21 | async-start | bytes 8912896 | tf_op jit(solution)/shard_map/all_gather | solution.py:110
  117.5 467.9 %all-gather.37.cloned.1.call-start = ((), (), s32[]{:S(2)}) async-start(), calls=%async_computation.22 | async-start | bytes 8912896 | tf_op jit(solution)/shard_map/all_gather | solution.py:111
  118.1 529.0 %all-gather.39.cloned.1.call-start = ((), (), s32[]{:S(2)}) async-start(), calls=%async_computation.23 | async-start | bytes 2228224 | tf_op jit(solution)/shard_map/all_gather | solution.py:112
  118.9 585.0 %all-gather.41.cloned.1.call-start = ((), (), s32[]{:S(2)}) async-start(), calls=%async_computation.24 | async-start | bytes 1114112 | tf_op jit(solution)/shard_map/all_gather | solution.py:113
  119.6 750.8 %all-gather.27.cloned.1.call-start = ((), (), s32[]{:S(2)}) async-start(), calls=%async_computation.11 | async-start | bytes 4456448 | tf_op jit(solution)/shard_map/all_gather | solution.py:315
  196.7 86.8 %copy-start.68 = (pred[2,64]{1,0:T(4,128)(4,1)}, pred[2,64]{1,0:T(4,128)(4,1)S(1)}, u32[]{:S(2)}) copy-start(pred[2,64]{1,0:T(4,128)(4,1)S(1)} %broadcast_compare_fusion) | copy-start | bytes 388
  235.0 41.8 %copy-start.24 = (bf16[1,16,512]{2,1,0:T(8,128)(2,1)}, bf16[1,16,512]{2,1,0:T(8,128)(2,1)S(1)}, u32[]{:S(2)}) copy-start(bf16[1,16,512]{2,1,0:T(8,128)(2,1)S(1)} %copy.162) | copy-start | bytes 49156
  277.2 607.9 %all-gather.29.cloned.1.call-start = ((), (), s32[]{:S(2)}) async-start(), calls=%async_computation.12 | async-start | bytes 4456448 | tf_op jit(solution)/shard_map/all_gather | solution.py:318
  287.3 11.4 copy-start.22
  292.5 6.3 copy-start.30
  307.0 164.7 %copy-start.19 = (bf16[128,1024]{1,0:T(8,128)(2,1)}, bf16[128,1024]{1,0:T(8,128)(2,1)S(1)}, u32[]{:S(2)}) copy-start(bf16[128,1024]{1,0:T(8,128)(2,1)S(1)} %convert_element_type.147) | copy-start | bytes 786436
  337.8 138.7 %copy-start.33 = (f32[128]{0:T(128)}, f32[128]{0:T(128)S(1)}, u32[]{:S(2)}) copy-start(f32[128]{0:T(128)S(1)} %broadcast_multiply_fusion.1) | copy-start | bytes 1540
  338.0 133.8 %copy-start.64 = (f32[128]{0:T(128)}, f32[128]{0:T(128)S(1)}, u32[]{:S(2)}) copy-start(f32[128]{0:T(128)S(1)} %multiply_reduce_fusion.5) | copy-start | bytes 1540
  338.0 138.5 %copy-start.36 = (f32[128]{0:T(128)}, f32[128]{0:T(128)S(1)}, u32[]{:S(2)}) copy-start(f32[128]{0:T(128)S(1)} %fusion.122) | copy-start | bytes 1540
  471.7 113.7 %copy-start.56 = (f32[1024]{0:T(1024)S(1)}, f32[1024]{0:T(1024)}, u32[]{:S(2)}) copy-start(f32[1024]{0:T(1024)} %get-tuple-element.86) | copy-start | bytes 12292
  591.7 117.5 %copy-start.3 = (f32[128,1024]{1,0:T(8,128)}, f32[128,1024]{1,0:T(8,128)S(1)}, u32[]{:S(2)}) copy-start(f32[128,1024]{1,0:T(8,128)S(1)} %fusion.83) | copy-start | bytes 1572868
  654.4 5.3 copy-start.45
  707.0 9.2 slice-start
  709.2 10.9 copy-start.7
  709.2 7.0 slice-start.1
  709.3 7.0 copy-start.34
  709.3 7.0 copy-start.37
  722.1 236.2 %reduce-scatter.26.cloned.1.call-start = ((), (), s32[]{:S(2)}) async-start(), calls=%async_computation.18 | async-start | bytes 2228224 | tf_op jit(solution)/shard_map/reduce_scatter | solution.py:152
  725.0 327.9 %reduce-scatter.18.cloned.1.call-start = ((), (), s32[]{:S(2)}) async-start(), calls=%async_computation.14 | async-start | bytes 4456448 | tf_op jit(solution)/shard_map/reduce_scatter | solution.py:148
  728.7 421.2 %reduce-scatter.24.cloned.1.call-start = ((), (), s32[]{:S(2)}) async-start(), calls=%async_computation.17 | async-start | bytes 4456448 | tf_op jit(solution)/shard_map/reduce_scatter | solution.py:151
  732.7 6.5 copy-start.23
  732.7 6.5 copy-start.31
  732.7 626.4 %reduce-scatter.16.cloned.1.call-start = ((), (), s32[]{:S(2)}) async-start(), calls=%async_computation.13 | async-start | bytes 13369344 | tf_op jit(solution)/shard_map/reduce_scatter | solution.py:147
  885.1 6.3 copy-start.69
  927.8 779.6 %reduce-scatter.20.cloned.1.call-start = ((), (), s32[]{:S(2)}) async-start(), calls=%async_computation.15 | async-start | bytes 17825792 | tf_op jit(solution)/shard_map/reduce_scatter | solution.py:149
  937.9 1123.8 %reduce-scatter.22.cloned.1.call-start = ((), (), s32[]{:S(2)}) async-start(), calls=%async_computation.16 | async-start | bytes 17825792 | tf_op jit(solution)/shard_map/reduce_scatter | solution.py:150
  947.1 1242.0 %reduce-scatter.30.cloned.1.call-start = ((), (), s32[]{:S(2)}) async-start(), calls=%async_computation.26 | async-start | bytes 278528
  948.9 1272.6 %reduce-scatter.32.cloned.1.call-start = ((), (), s32[]{:S(2)}) async-start(), calls=%async_computation.27 | async-start | bytes 278528
  950.0 5.1 copy-start.39
  950.0 1347.3 %reduce-scatter.28.cloned.1.call-start = ((), (), s32[]{:S(2)}) async-start(), calls=%async_computation.25 | async-start | bytes 557056
  954.0 1107.6 %copy-start.46 = (f32[128]{0:T(128)S(1)}, f32[128]{0:T(128)}, u32[]{:S(2)}) copy-start(f32[128]{0:T(128)} %copy-done.45) | copy-start | bytes 1540
  954.0 1107.6 %copy-start.51 = (f32[128]{0:T(128)S(1)}, f32[128]{0:T(128)}, u32[]{:S(2)}) copy-start(f32[128]{0:T(128)} %copy-done.50) | copy-start | bytes 1540
  954.1 1154.7 %copy-start.14 = (f32[128,512]{1,0:T(8,128)S(1)}, f32[128,512]{1,0:T(8,128)}, u32[]{:S(2)}) copy-start(f32[128,512]{1,0:T(8,128)} %copy-done.13) | copy-start | bytes 786436
  954.1 1155.7 %copy-start.43 = (f32[4096]{0:T(1024)S(1)}, f32[4096]{0:T(1024)}, u32[]{:S(2)}) copy-start(f32[4096]{0:T(1024)} %get-tuple-element.139) | copy-start | bytes 49156
  954.1 1233.6 %copy-start.4 = (f32[128,1024]{1,0:T(8,128)S(1)}, f32[128,1024]{1,0:T(8,128)}, u32[]{:S(2)}) copy-start(f32[128,1024]{1,0:T(8,128)} %copy-done.3) | copy-start | bytes 1572868
  954.1 1233.6 %copy-start.6 = (f32[128,512]{1,0:T(8,128)S(1)}, f32[128,512]{1,0:T(8,128)}, u32[]{:S(2)}) copy-start(f32[128,512]{1,0:T(8,128)} %copy-done.5) | copy-start | bytes 786436
  954.1 1233.6 %copy-start.11 = (bf16[1,512,1024]{1,2,0:T(8,128)(2,1)S(1)}, bf16[1,512,1024]{1,2,0:T(8,128)(2,1)}, u32[]{:S(2)}) copy-start(bf16[1,512,1024]{1,2,0:T(8,128)(2,1)} %all-gather.41.cloned.1.call-done) | copy-start | bytes 3145732
  954.1 1233.6 %copy-start.44 = (f32[1024]{0:T(1024)S(1)}, f32[1024]{0:T(1024)}, u32[]{:S(2)}) copy-start(f32[1024]{0:T(1024)} %get-tuple-element.85) | copy-start | bytes 12292
  955.1 1267.2 %copy-start.61 = (f32[128]{0:T(128)S(1)}, f32[128]{0:T(128)}, u32[]{:S(2)}) copy-start(f32[128]{0:T(128)} %get-tuple-element.81) | copy-start | bytes 1540
  955.1 1267.2 %copy-start.58 = (f32[128]{0:T(128)S(1)}, f32[128]{0:T(128)}, u32[]{:S(2)}) copy-start(f32[128]{0:T(128)} %copy-done.57) | copy-start | bytes 1540
  956.3 1364.3 %all-reduce.8.cloned.1.call-start = ((), (), s32[]{:S(2)}) async-start(), calls=%async_computation.28 | async-start | bytes 7077888 | tf_op jit(solution)/shard_map/psum | solution.py:158
  2320.6 6.1 copy-start.20
  2320.6 7.1 copy-start.21
  2320.6 7.8 copy-start.28
  (28 other events, 77.2 us)
Sparse Core Ops, SparseCore 0:
  10.8 98.8 all-gather.30
  115.6 75.8 all-gather.24
  194.9 78.3 all-gather.22
  275.9 59.3 all-gather.32
  337.8 133.8 all-gather.34
  474.4 111.0 all-gather.36
  588.2 58.8 all-gather.38
  649.9 53.9 all-gather.40
  706.6 80.5 all-gather.26
  789.8 87.4 all-gather.28
  879.5 78.7 reduce-scatter.25
  960.4 92.4 reduce-scatter.17
  1055.2 94.7 reduce-scatter.23
  1155.4 203.6 reduce-scatter.15
  1361.3 345.9 reduce-scatter.19
  1709.6 351.9 reduce-scatter.21
  2064.4 81.8 reduce-scatter.29
  2149.0 72.4 reduce-scatter.31
  2224.4 72.8 reduce-scatter.27
  2299.9 20.6 all-reduce.7
where the time goes:
time: 2350 us; the launch traced here: 2340 us
  waiting for transfers between devices  1620 us (69%)
  blocking collectives  429 us (18%)
  matrix products  135 us (6%)
  local copies, waits for them, and re-layouts  111 us (5%)
  other arithmetic  24.9 us (1%)
    reduce_scatter x1, waiting for transfers between devices, reduce_grads(): lax.psum_scatter(grad_back_w, 'blk', scatter_dimension=1, tiled=True)  354 us
    reduce_scatter x1, waiting for transfers between devices, reduce_grads(): lax.psum_scatter(grad_in_w, 'blk', scatter_dimension=1, tiled=True)  348 us
    reduce_scatter x1, waiting for transfers between devices, reduce_grads(): lax.psum_scatter(grad_qkv_w, 'blk', scatter_dimension=1, tiled=True)  209 us
    unnamed x2, blocking collectives  152 us
    all_gather x1, waiting for transfers between devices, gather_weights(): lax.all_gather(part_in, 'blk', axis=1, tiled=True)  134 us
    unnamed x23, waiting for transfers between devices  109 us
    all_gather x1, waiting for transfers between devices, gather_weights(): lax.all_gather(part_back, 'blk', axis=1, tiled=True)  109 us
    reduce_scatter x1, waiting for transfers between devices, reduce_grads(): lax.psum_scatter(grad_latent_w, 'blk', scatter_dimension=1, tiled=True)  97 us
  transfers between devices with their start and end apart: 20, of which 15 were waited for; matrix products, arithmetic and copies ran while one was open for 11% of the time, Pallas kernels for 0%

commit v1 on v0

--- a/solution.py
+++ b/solution.py
@@ -2,7 +2,11 @@
 
 import jax
 import jax.numpy as jnp
+import numpy as np
 from jax import lax
+from jax.experimental import pallas as pl
+from jax.experimental.pallas import tpu as pltpu
+from jax.sharding import Mesh
 from jax.sharding import PartitionSpec as P
 
 HEADS = 16
@@ -477,41 +481,680 @@
     )
 
 
+ZY = ("z", "y")
+CHIPS = ("z", "y", "x")
+EVERY = ("grp", "z", "y", "x")
+PAIR = 2 * HEAD_DIM
+VMEM_LIMIT = 48 * 1024 * 1024
+
+
+def hop(values, axis, step=1):
+    size = lax.axis_size(axis)
+    return lax.ppermute(values, axis, [(i, i ^ step) for i in range(size)])
+
+
+def other_core(values):
+    return hop(values, "grp")
+
+
+def swap_groups(values):
+    return lax.ppermute(values, ("grp", "x"), [(0, 0), (1, 2), (2, 1), (3, 3)])
+
+
+def by_core(own, other, axis):
+    first = lax.axis_index("grp") == 0
+    return jnp.concatenate(
+        [jnp.where(first, own, other), jnp.where(first, other, own)], axis=axis
+    )
+
+
+def half_of(values, axis, mine):
+    part = values.shape[axis] // 2
+    core = lax.axis_index("grp")
+    place = core if mine else 1 - core
+    return lax.dynamic_slice_in_dim(values, place * part, part, axis)
+
+
+def flip(place, step):
+    high = (place // 2 + step // 2) % 2
+    low_bit = (place % 2 + step % 2) % 2
+    return high * 2 + low_bit
+
+
+PLAN_A = (
+    (0, 32, 0, 0, 512, 0, 64, 0, 0),
+    (0, 32, 1, 0, 512, 0, 64, 32, 0),
+    (32, 128, 0, 0, 512, 1, 128, 0, 0),
+    (32, 128, 1, 0, 512, 1, 128, 0, 512),
+)
+SHAPES_A = ((1024, 512), (2048, 1024))
+PLAN_B = (
+    (0, 64, 0, 0, 512, 0, 64, 0, 0),
+    (0, 64, 1, 0, 512, 0, 64, 0, 512),
+    (64, 64, 0, 0, 512, 0, 64, 0, 1024),
+    (64, 64, 1, 0, 512, 0, 64, 0, 1536),
+    (128, 32, 0, 0, 512, 1, 64, 0, 0),
+    (128, 32, 1, 0, 512, 1, 64, 32, 0),
+    (160, 16, 0, 0, 256, 2, 64, 0, 0),
+    (160, 16, 0, 256, 256, 2, 64, 16, 0),
+    (160, 16, 1, 0, 256, 2, 64, 32, 0),
+    (160, 16, 1, 256, 256, 2, 64, 48, 0),
+)
+SHAPES_B = ((1024, 2048), (1024, 512), (1024, 256))
+PLAN_C = (
+    (0, 96, 0, 0, 512, 0, 192, 0, 0),
+    (0, 96, 1, 0, 512, 0, 192, 96, 0),
+)
+SHAPES_C = ((3072, 512),)
+BLOCKS = [(dz, dy, dx) for dz in range(4) for dy in range(2) for dx in range(2)]
+
+
+def run_copies(copies, sems):
+    started = []
+    for place, (source, target) in enumerate(copies):
+        copy = pltpu.make_async_copy(source, target, sems.at[place])
+        copy.start()
+        started.append(copy)
+    for copy in started:
+        copy.wait()
+
+
+def copy_call(body, operands, out_shapes, count):
+    anywhere = pl.BlockSpec(memory_space=pl.ANY)
+    return pl.pallas_call(
+        body,
+        out_shape=out_shapes,
+        in_specs=[anywhere] * len(operands),
+        out_specs=[pl.BlockSpec(memory_space=pltpu.VMEM)] * len(out_shapes),
+        scratch_shapes=[pltpu.SemaphoreType.DMA((count,))],
+        compiler_params=pltpu.CompilerParams(vmem_limit_bytes=VMEM_LIMIT),
+    )(*operands)
+
+
+def block_rows(entry, step):
+    dz, dy, dx = step
+    block = (
+        flip(lax.axis_index("z"), dz) * 2 + flip(lax.axis_index("y"), dy)
+    ) * 2 + flip(lax.axis_index("x"), dx)
+    return pl.multiple_of(block * entry[6] + entry[7], 16)
+
+
+def gather_group(shard, plan, shapes):
+    parts = jnp.stack([shard] + [hop(shard, "z", step) for step in (1, 2, 3)])
+    left, right = parts[:, :, :512], parts[:, :, 512:]
+    left_x = hop(left, "x")
+    right_y = hop(right, "y")
+    left_two = jnp.stack([left, left_x])
+    right_two = jnp.stack([right, right_y])
+    left_far = hop(left_two, "y")
+    right_far = hop(right_two, "x")
+
+    def body(left_near, left_off, right_near, right_off, *rest):
+        outs, sems = rest[:-1], rest[-1]
+        copies = []
+        for step in BLOCKS:
+            dz, dy, dx = step
+            for entry in plan:
+                row, rows, side, lane, lanes, array, _, _, to_lane = entry
+                if side == 0:
+                    source = (left_off if dy else left_near).at[dx, dz]
+                else:
+                    source = (right_off if dx else right_near).at[dy, dz]
+                copies.append(
+                    (
+                        source.at[pl.ds(row, rows), pl.ds(lane, lanes)],
+                        outs[array].at[pl.ds(block_rows(entry, step), rows), pl.ds(to_lane, lanes)],
+                    )
+                )
+        run_copies(copies, sems)
+
+    return copy_call(
+        body,
+        (left_two, left_far, right_two, right_far),
+        [jax.ShapeDtypeStruct(shape, shard.dtype) for shape in shapes],
+        len(BLOCKS) * len(plan),
+    )
+
+
+def scatter_group(grads, plan, rows_all):
+    def body(*refs):
+        sources, (left_keep, left_send, right_keep, right_send), sems = (
+            refs[: len(grads)],
+            refs[len(grads) : -1],
+            refs[-1],
+        )
+        copies = []
+        for step in BLOCKS:
+            dz, dy, dx = step
+            for entry in plan:
+                row, rows, side, lane, lanes, array, _, _, at_lane = entry
+                if side == 0:
+                    target = (left_send if dx else left_keep).at[dy, dz]
+                else:
+                    target = (right_send if dy else right_keep).at[dx, dz]
+                copies.append(
+                    (
+                        sources[array].at[
+                            pl.ds(block_rows(entry, step), rows), pl.ds(at_lane, lanes)
+                        ],
+                        target.at[pl.ds(row, rows), pl.ds(lane, lanes)],
+                    )
+                )
+        run_copies(copies, sems)
+
+    piece = jax.ShapeDtypeStruct((2, 4, rows_all, 512), jnp.bfloat16)
+    left_keep, left_send, right_keep, right_send = copy_call(
+        body, grads, [piece] * 4, len(BLOCKS) * len(plan)
+    )
+    left_came = hop(left_send, "x")
+    right_came = hop(right_send, "y")
+    left_sum = left_keep.astype(jnp.float32) + left_came.astype(jnp.float32)
+    right_sum = right_keep.astype(jnp.float32) + right_came.astype(jnp.float32)
+    left_last = hop(to_low(left_sum[1]), "y")
+    right_last = hop(to_low(right_sum[1]), "x")
+    whole = jnp.concatenate(
+        [
+            left_sum[0] + left_last.astype(jnp.float32),
+            right_sum[0] + right_last.astype(jnp.float32),
+        ],
+        axis=2,
+    )
+    travel = to_low(whole)
+    total = whole[0]
+    for step in (1, 2, 3):
+        total = total + hop(travel[step], "z", step).astype(jnp.float32)
+    return total
+
+
+def side_by_side(rows, count):
+    part = rows.shape[0] // count
+    return jnp.concatenate([rows[i * part : (i + 1) * part] for i in range(count)], axis=1)
+
+
+def one_below(rows, count):
+    part = rows.shape[1] // count
+    return jnp.concatenate([rows[:, i * part : (i + 1) * part] for i in range(count)], axis=0)
+
+
+def place_cells(near, far):
+    rows = near.shape[1] - 16
+
+    def body(near_ref, far_ref, cells_ref, small_ref, sems):
+        copies = []
+        for dz in range(4):
+            for dy, ref in ((0, near_ref), (1, far_ref)):
+                block = flip(lax.axis_index("z"), dz) * 2 + flip(lax.axis_index("y"), dy)
+                copies.append((ref.at[dz, pl.ds(0, rows)], cells_ref.at[block]))
+                copies.append((ref.at[dz, pl.ds(rows, 16)], small_ref.at[block]))
+        run_copies(copies, sems)
+
+    width = near.shape[2]
+    return copy_call(
+        body,
+        (near, far),
+        [
+            jax.ShapeDtypeStruct((8, rows, width), near.dtype),
+            jax.ShapeDtypeStruct((8, 16, width), near.dtype),
+        ],
+        16,
+    )
+
+
+def head_lanes(rows):
+    return lax.broadcasted_iota(jnp.int32, (rows, PAIR), 1) < HEAD_DIM
+
+
+def attend_body(own_ref, other_ref, bias_ref, mixed_ref, lse_ref):
+    rows = own_ref.shape[0] * own_ref.shape[2]
+    own = own_ref[...].reshape(rows, 3 * PAIR)
+    other = other_ref[...].reshape(rows, 2 * PAIR)
+    keys = jnp.concatenate([own[:, PAIR : 2 * PAIR], other[:, :PAIR]], axis=0)
+    values = jnp.concatenate([own[:, 2 * PAIR :], other[:, PAIR:]], axis=0)
+    bias = bias_ref[0]
+    step = 256
+    first_head = head_lanes(step)
+    for start in range(0, rows, step):
+        query = own[start : start + step, :PAIR]
+        outs, totals = [], []
+        for head in range(2):
+            mine = first_head if head == 0 else jnp.logical_not(first_head)
+            part = jnp.where(mine, query, jnp.zeros_like(query))
+            scores = product_nt(part, keys) + bias
+            peak = jnp.max(scores, axis=-1, keepdims=True)
+            weights = jnp.exp(scores - peak)
+            total = jnp.sum(weights, axis=-1, keepdims=True)
+            outs.append(product(to_low(weights / total), values))
+            totals.append(jnp.broadcast_to(peak + jnp.log(total), (step, PAIR)))
+        mixed = to_low(jnp.where(first_head, outs[0], outs[1]))
+        span = mixed_ref.shape[2]
+        mixed_ref[start // span : (start + step) // span, 0] = mixed.reshape(
+            step // span, span, PAIR
+        )
+        lse_ref[0, start : start + step] = jnp.where(first_head, totals[0], totals[1])
+
+
+def slot_block(shape):
+    return pl.BlockSpec((shape[0], 1) + tuple(shape[2:]), lambda s: (0, s, 0, 0))
+
+
+def plane_block(shape):
+    return pl.BlockSpec((1,) + tuple(shape[1:]), lambda s: (s, 0, 0))
+
+
+def attend(qkv_own, kv_other, bias):
+    blocks, slots, span, _ = qkv_own.shape
+    rows = blocks * span
+    mixed_shape = (blocks, slots, span, PAIR)
+    lse_shape = (slots, rows, PAIR)
+    return pl.pallas_call(
+        attend_body,
+        grid=(slots,),
+        in_specs=[slot_block(qkv_own.shape), slot_block(kv_other.shape), plane_block(bias.shape)],
+        out_specs=[slot_block(mixed_shape), plane_block(lse_shape)],
+        out_shape=[
+            jax.ShapeDtypeStruct(mixed_shape, jnp.bfloat16),
+            jax.ShapeDtypeStruct(lse_shape, jnp.float32),
+        ],
+        compiler_params=pltpu.CompilerParams(vmem_limit_bytes=VMEM_LIMIT),
+    )(qkv_own, kv_other, bias)
+
+
+def attend_back_body(
+    own_ref, other_ref, bias_ref, lse_ref, dmixed_ref, dquery_ref, down_ref, dother_ref, dk_ref, dv_ref
+):
+    rows = own_ref.shape[0] * own_ref.shape[2]
+    own = own_ref[...].reshape(rows, 3 * PAIR)
+    other = other_ref[...].reshape(rows, 2 * PAIR)
+    keys = jnp.concatenate([own[:, PAIR : 2 * PAIR], other[:, :PAIR]], axis=0)
+    values = jnp.concatenate([own[:, 2 * PAIR :], other[:, PAIR:]], axis=0)
+    dmixed_all = dmixed_ref[...].reshape(rows, PAIR)
+    bias = bias_ref[0]
+    step = 256
+    first_head = head_lanes(step)
+    for start in range(0, rows, step):
+        query = own[start : start + step, :PAIR]
+        dmixed = dmixed_all[start : start + step]
+        dqueries = []
+        dkeys = jnp.zeros((2 * rows, PAIR), jnp.float32)
+        dvalues = jnp.zeros((2 * rows, PAIR), jnp.float32)
+        for head in range(2):
+            mine = first_head if head == 0 else jnp.logical_not(first_head)
+            part = jnp.where(mine, query, jnp.zeros_like(query))
+            dpart = jnp.where(mine, dmixed, jnp.zeros_like(dmixed))
+            lse = lse_ref[0, start : start + step, head * HEAD_DIM : head * HEAD_DIM + 1]
+            probs = jnp.exp(product_nt(part, keys) + bias - lse)
+            dprobs = product_nt(dpart, values)
+            centre = jnp.sum(dprobs * probs, axis=-1, keepdims=True)
+            dscores = to_low(probs * (dprobs - centre))
+            dqueries.append(product(dscores, keys))
+            dkeys = dkeys + product_tn(dscores, part)
+            dvalues = dvalues + product_tn(to_low(probs), dpart)
+        span = dquery_ref.shape[2]
+        dquery = to_low(jnp.where(first_head, dqueries[0], dqueries[1]) * (HEAD_DIM**-0.5))
+        dquery_ref[start // span : (start + step) // span, 0] = dquery.reshape(
+            step // span, span, PAIR
+        )
+        if start == 0:
+            dk_ref[...] = dkeys
+            dv_ref[...] = dvalues
+        else:
+            dk_ref[...] += dkeys
+            dv_ref[...] += dvalues
+    grid = (own_ref.shape[0], own_ref.shape[2], PAIR)
+    down_ref[:, 0, :, :PAIR] = dk_ref[:rows].reshape(grid)
+    down_ref[:, 0, :, PAIR:] = dv_ref[:rows].reshape(grid)
+    dother_ref[:, 0, :, :PAIR] = dk_ref[rows:].reshape(grid)
+    dother_ref[:, 0, :, PAIR:] = dv_ref[rows:].reshape(grid)
+
+
+def attend_back(qkv_own, kv_other, bias, lse, dmixed):
+    blocks, slots, span, _ = qkv_own.shape
+    rows = blocks * span
+    dkv = (blocks, slots, span, 2 * PAIR)
+    return pl.pallas_call(
+        attend_back_body,
+        grid=(slots,),
+        in_specs=[
+            slot_block(qkv_own.shape),
+            slot_block(kv_other.shape),
+            plane_block(bias.shape),
+            plane_block(lse.shape),
+            slot_block(dmixed.shape),
+        ],
+        out_specs=[slot_block(dmixed.shape), slot_block(dkv), slot_block(dkv)],
+        out_shape=[
+            jax.ShapeDtypeStruct(dmixed.shape, jnp.bfloat16),
+            jax.ShapeDtypeStruct(dkv, jnp.float32),
+            jax.ShapeDtypeStruct(dkv, jnp.float32),
+        ],
+        scratch_shapes=[
+            pltpu.VMEM((2 * rows, PAIR), jnp.float32),
+            pltpu.VMEM((2 * rows, PAIR), jnp.float32),
+        ],
+        compiler_params=pltpu.CompilerParams(vmem_limit_bytes=VMEM_LIMIT),
+    )(qkv_own, kv_other, bias, lse, dmixed)
+
+
+def head_routes(index):
+    routes = []
+    for core in range(2):
+        for chip in range(16):
+            head = (3 * chip + index) % 16
+            routes.append((core * 16 + chip, (head % 2) * 16 + (head // 2) * 2 + core))
+    return routes
+
+
+def head_roles():
+    roles = np.zeros((16, 3), np.int32)
+    for chip in range(16):
+        for index in range(3):
+            block = 3 * chip + index
+            roles[block % 16, block // 16] = index
+    return roles
+
+
+def fast_device(
+    cell_input,
+    lengths,
+    noise_draw,
+    cotangent,
+    w_qkv,
+    w_out,
+    w_ffn_in,
+    w_ffn_out,
+    w_latent,
+    w_decode,
+    vectors,
+    inner_bias,
+    prior_means,
+    prior_logvars,
+):
+    slots, span, width = cell_input.shape[1:]
+    rows = slots * span
+    lat = noise_draw.shape[-1]
+    comps = prior_means.shape[1]
+    ff = w_ffn_out.shape[1]
+    core, zi, yi = lax.axis_index("grp"), lax.axis_index("z"), lax.axis_index("y")
+    pair = zi * 2 + yi
+    head = pair * 2 + core
+    low = jnp.bfloat16
+
+    pad = jnp.zeros((width,), low)
+    lens = lengths[0]
+    lens_low = jnp.concatenate([lens // 32, lens % 32]).astype(low)
+    small_rows = jnp.stack(
+        [
+            jnp.concatenate([vectors.reshape(-1), inner_bias.reshape(-1), pad])[:width],
+            jnp.concatenate([prior_means.reshape(-1), prior_logvars.reshape(-1)]),
+            jnp.concatenate([lens_low, pad])[:width],
+        ]
+        + [pad] * 13
+    )
+    first = swap_groups(jnp.concatenate([cell_input[0].reshape(rows, width), small_rows]))
+    near = [first] + [hop(first, "z", step) for step in (1, 2, 3)]
+    far = [hop(block, "y") for block in near]
+    cells, small_own = place_cells(jnp.stack(near), jnp.stack(far))
+    small_other = other_core(small_own)
+
+    qkv_t = w_qkv[0].T.reshape(3, HEAD_DIM, width)
+    came = jnp.stack([lax.ppermute(qkv_t[i], EVERY, head_routes(i)) for i in range(3)])
+    roles = jnp.asarray(head_roles())[head]
+    head_w = jnp.stack([lax.dynamic_index_in_dim(came, roles[j], 0, False) for j in range(3)])
+    head_w_other = other_core(head_w)
+    pair_w = by_core(head_w[:, None], head_w_other[:, None], 1).reshape(3 * PAIR, width)
+
+    shard_out = side_by_side(half_of(w_out[0], 0, True).T, 2)
+    shard_in = half_of(w_ffn_in[0], 1, True).T
+    back_rows = half_of(w_ffn_out[0].reshape(16, 2, ff // 32, -1), 1, True)
+    shard_back = one_below(back_rows.reshape(ff // 2, -1).T, 2)
+    shard_lat = side_by_side(half_of(w_latent[0], 0, True).T, 2)
+    shard_dec = side_by_side(half_of(w_decode[0], 0, True).T, 4)
+    shard_qkv = side_by_side(half_of(w_qkv[0], 0, True).T, 2)
+    out_t, in_t = gather_group(jnp.concatenate([shard_out, shard_in]), PLAN_A, SHAPES_A)
+    back_t, lat_t, dec_t = gather_group(
+        jnp.concatenate([shard_back, shard_lat, shard_dec]), PLAN_B, SHAPES_B
+    )
+    (qkv_all_t,) = gather_group(shard_qkv, PLAN_C, SHAPES_C)
+    out_t_other, lat_t_other = other_core(out_t), other_core(lat_t)
+    dec_t_other, qkv_all_t_other = other_core(dec_t), other_core(qkv_all_t)
+
+    def full_nt(left, own, other):
+        return product_nt(half_of(left, 1, True), own) + product_nt(
+            half_of(left, 1, False), other
+        )
+
+    def full_nn(left, own, other):
+        return by_core(product(left, own), product(left, other), 1)
+
+    small = by_core(small_own[:, None], small_other[:, None], 1).reshape(16, 16, width)
+    small = small.astype(jnp.float32)
+    n_vec = 9 * (width // 16)
+    vec_rows = small[:, 0, :n_vec].reshape(16, 9, width // 16)
+    vec_rows = vec_rows.transpose(1, 0, 2).reshape(9, width)
+    inner_part = small[:, 0, n_vec : n_vec + inner_bias.shape[1]].reshape(-1)
+    mean_rows = small[:, 1, :lat].reshape(16, comps, lat // 16)
+    mean_rows = mean_rows.transpose(1, 0, 2).reshape(comps, lat)
+    logvars = small[:, 1, lat:].reshape(16, comps, lat // 16)
+    logvars = logvars.transpose(1, 0, 2).reshape(comps, lat)
+    lens_f = first[rows + 2, : 2 * slots].astype(jnp.float32)
+    slide_len = (lens_f[:slots] * 32 + lens_f[slots:]).astype(jnp.int32)
+    ff_bias = half_of(inner_part[:ff].reshape(16, 2, ff // 32), 1, True).reshape(ff // 2)
+    lat_bias = inner_part[ff:]
+
+    cells_f = cells.reshape(8 * rows, width).astype(jnp.float32)
+    normed = to_low(layer_norm(cells_f, vec_rows[0], vec_rows[1]))
+    pair_q = lax.dynamic_slice_in_dim(vec_rows[2], pair * PAIR, PAIR)
+    pair_v = lax.dynamic_slice_in_dim(vec_rows[3], pair * PAIR, PAIR)
+    qkv = product_nt(normed, pair_w)
+    query = to_low(qkv[:, :PAIR] + pair_q) * jnp.asarray(HEAD_DIM**-0.5, low)
+    qkv_own = jnp.concatenate(
+        [query, to_low(qkv[:, PAIR : 2 * PAIR]), to_low(qkv[:, 2 * PAIR :] + pair_v)], axis=1
+    ).reshape(8, slots, span, 3 * PAIR)
+    kv_other = other_core(qkv_own[..., PAIR:])
+    starts = jnp.arange(8)[None, :] * 2 + jnp.stack([core, 1 - core])[:, None]
+    places = (starts[:, :, None] * span + jnp.arange(span)).reshape(-1)
+    bias = jnp.where(places[None, :] < slide_len[:, None], 0.0, MASKED)[:, None, :]
+    mixed_pair, lse = attend(qkv_own, kv_other, bias)
+    mixed_low = lax.all_to_all(
+        mixed_pair.reshape(8, rows, PAIR), ZY, split_axis=0, concat_axis=0, tiled=True
+    )
+    mixed_low = mixed_low.transpose(1, 0, 2).reshape(rows, width)
+
+    hidden = first[:rows].astype(jnp.float32)
+    noise_rows = swap_groups(noise_draw.reshape(rows, lat))
+    cot_low = swap_groups(cotangent.reshape(rows, width))
+    row_places = head * span + jnp.arange(span)
+    live_rows = (row_places[None, :] < slide_len[:, None]).reshape(rows)
+    attended = hidden + full_nt(mixed_low, out_t, out_t_other) + vec_rows[4]
+    normed_two = to_low(layer_norm(attended, vec_rows[5], vec_rows[6]))
+    both_two = jnp.concatenate([normed_two, other_core(normed_two)])
+    inner_act = product_nt(both_two, in_t) + ff_bias
+    activated = to_low(jax.nn.gelu(inner_act))
+    fed_parts = product_nt(activated, back_t)
+    fed_rows = attended + (fed_parts[:rows] + other_core(fed_parts[rows:])) + vec_rows[7]
+    fed_low = to_low(fed_rows)
+    latent = full_nt(fed_low, lat_t, lat_t_other) + lat_bias
+
+    def bottle(latent_in, means_in, logvars_in):
+        return bottleneck(latent_in, noise_rows, live_rows, means_in, logvars_in)
+
+    (sample, kl_part), bottle_pull = jax.vjp(bottle, latent, mean_rows, logvars)
+    sample_low = to_low(sample)
+    output = fed_rows + full_nt(sample_low, dec_t, dec_t_other) + vec_rows[8]
+    layer_out = swap_groups(output)
+
+    grad_out = cot_low.astype(jnp.float32)
+    grad_sample = full_nn(cot_low, dec_t, dec_t_other)
+    grad_latent_f, grad_mean_rows, grad_logvars = bottle_pull(
+        (grad_sample, jnp.ones((), jnp.float32))
+    )
+    grad_latent_low = to_low(grad_latent_f)
+    grad_fed = grad_out + full_nn(grad_latent_low, lat_t, lat_t_other)
+    grad_fed_low = to_low(grad_fed)
+    both_fed = jnp.concatenate([grad_fed_low, other_core(grad_fed_low)])
+    grad_act = product(both_fed, back_t)
+    ignored, gelu_pull = jax.vjp(jax.nn.gelu, inner_act)
+    grad_inner_low = to_low(gelu_pull(grad_act)[0])
+    norm_parts = product(grad_inner_low, in_t)
+    grad_normed_two = norm_parts[:rows] + other_core(norm_parts[rows:])
+    ignored, second_pull = jax.vjp(layer_norm, attended, vec_rows[5], vec_rows[6])
+    grad_att_norm, grad_gain_two, grad_shift_two = second_pull(grad_normed_two)
+    grad_attended = grad_fed + grad_att_norm
+    grad_proj_low = to_low(grad_attended)
+    grad_mixed_low = to_low(full_nn(grad_proj_low, out_t, out_t_other))
+    dmixed = lax.all_to_all(
+        grad_mixed_low.reshape(rows, 8, PAIR).transpose(1, 0, 2),
+        ZY,
+        split_axis=0,
+        concat_axis=0,
+        tiled=True,
+    ).reshape(8, slots, span, PAIR)
+
+    def weight_grad(left, right):
+        return to_low(product_tn(left, right))
+
+    both_cot = jnp.concatenate([cot_low, other_core(cot_low)])
+    both_sample = jnp.concatenate([sample_low, other_core(sample_low)])
+    both_lat = jnp.concatenate([grad_latent_low, other_core(grad_latent_low)])
+    both_fed_low = jnp.concatenate([fed_low, other_core(fed_low)])
+    both_proj = jnp.concatenate([grad_proj_low, other_core(grad_proj_low)])
+    both_mixed = jnp.concatenate([mixed_low, other_core(mixed_low)])
+    sum_b = scatter_group(
+        (
+            weight_grad(both_fed, activated),
+            weight_grad(both_lat, half_of(both_fed_low, 1, True)),
+            weight_grad(both_cot, half_of(both_sample, 1, True)),
+        ),
+        PLAN_B,
+        176,
+    )
+    sum_a = scatter_group(
+        (
+            weight_grad(both_proj, half_of(both_mixed, 1, True)),
+            weight_grad(grad_inner_low, both_two),
+        ),
+        PLAN_A,
+        160,
+    )
+
+    dquery, dkv_own, dkv_other = attend_back(qkv_own, kv_other, bias, lse, dmixed)
+    dkv = to_low(dkv_own + other_core(dkv_other))
+    dqkv = jnp.concatenate([dquery, dkv], axis=3).reshape(8, rows, 3 * PAIR)
+    dqkv_rows = lax.all_to_all(dqkv, ZY, split_axis=0, concat_axis=0, tiled=True)
+    dqkv_rows = dqkv_rows.reshape(8, rows, 3, PAIR).transpose(2, 1, 0, 3).reshape(3, rows, width)
+    grad_query_low, grad_keys_low, grad_values_low = dqkv_rows
+    grad_normed = full_nn(
+        jnp.concatenate([grad_query_low, grad_keys_low, grad_values_low], axis=1),
+        qkv_all_t,
+        qkv_all_t_other,
+    )
+    ignored, first_pull = jax.vjp(layer_norm, hidden, vec_rows[0], vec_rows[1])
+    grad_hid_norm, grad_gain_one, grad_shift_one = first_pull(grad_normed)
+    grad_cells = swap_groups(grad_attended + grad_hid_norm)
+
+    pair_grad = product_tn(dqkv.reshape(8 * rows, 3 * PAIR), normed)
+    pair_grad = pair_grad.reshape(3, 2, HEAD_DIM, width)
+    head_grad = half_of(pair_grad, 1, True) + other_core(half_of(pair_grad, 1, False))
+    head_grad = to_low(head_grad.reshape(3, HEAD_DIM, width))
+    places_of = jnp.argsort(roles)
+    back_home = [
+        lax.ppermute(
+            lax.dynamic_index_in_dim(head_grad, places_of[i], 0, False),
+            EVERY,
+            [(there, here) for here, there in head_routes(i)],
+        )
+        for i in range(3)
+    ]
+    home_grad = jnp.concatenate(back_home)
+    grad_qkv = (
+        home_grad.astype(jnp.float32) + other_core(home_grad).astype(jnp.float32)
+    ).T
+
+    grad_vec = jnp.stack(
+        [
+            grad_gain_one,
+            grad_shift_one,
+            jnp.sum(grad_query_low.astype(jnp.float32), axis=0),
+            jnp.sum(grad_values_low.astype(jnp.float32), axis=0),
+            jnp.sum(grad_attended, axis=0),
+            grad_gain_two,
+            grad_shift_two,
+            jnp.sum(grad_fed, axis=0),
+            jnp.sum(grad_out, axis=0),
+        ]
+    )
+    ff_own = jnp.sum(grad_inner_low.astype(jnp.float32), axis=0).reshape(16, 1, ff // 32)
+    ff_sums = by_core(ff_own, jnp.zeros_like(ff_own), 1).reshape(16, ff // 16)
+    lat_sums = jnp.sum(grad_latent_low.astype(jnp.float32), axis=0)
+    inner_sums = jnp.concatenate([ff_sums.reshape(-1), lat_sums]).reshape(16, -1)
+    small_sums = jnp.concatenate(
+        [
+            grad_vec.reshape(9, 16, -1).transpose(1, 0, 2).reshape(16, -1),
+            inner_sums,
+            grad_mean_rows.reshape(comps, 16, -1).transpose(1, 0, 2).reshape(16, -1),
+            grad_logvars.reshape(comps, 16, -1).transpose(1, 0, 2).reshape(16, -1),
+            jnp.broadcast_to(kl_part, (16, 128)),
+        ],
+        axis=1,
+    )
+    small_width = small_sums.shape[1]
+    small_sums = lax.all_to_all(
+        small_sums.reshape(16, small_width // 128, 128),
+        CHIPS,
+        split_axis=0,
+        concat_axis=0,
+        tiled=True,
+    )
+    small_sums = jnp.sum(small_sums, axis=0)
+    small_sums = (small_sums + other_core(small_sums)).reshape(-1)
+    cuts = np.cumsum([n_vec, inner_sums.shape[1], comps * lat // 16, comps * lat // 16])
+    vec_out, inner_out, means_out, logvars_out, kl_out = jnp.split(small_sums, cuts)
+    kl_mean = kl_out[0] / (32 * rows)
+
+    other_a, other_b = other_core(sum_a), other_core(sum_b)
+
+    def halves(pick, axis):
+        return by_core(pick(sum_a, sum_b), pick(other_a, other_b), axis)
+
+    grad_out_w = halves(lambda a, b: one_below(a[:32], 2).T, 0)
+    grad_in_w = halves(lambda a, b: a[32:].T, 1)
+    grad_back_w = halves(
+        lambda a, b: side_by_side(b[:128], 2).T.reshape(16, 1, ff // 32, -1), 1
+    ).reshape(ff, -1)
+    grad_lat_w = halves(lambda a, b: one_below(b[128:160], 2).T, 0)
+    grad_dec_w = halves(lambda a, b: one_below(b[160:], 4).T, 0)
+    return (
+        layer_out.reshape(1, slots, span, width),
+        grad_cells.reshape(1, slots, span, width),
+        kl_mean,
+        grad_qkv[None],
+        grad_out_w[None],
+        grad_in_w[None],
+        grad_back_w[None],
+        grad_lat_w[None],
+        grad_dec_w[None],
+        vec_out.reshape(1, 9, -1),
+        inner_out[None],
+        means_out.reshape(1, comps, -1),
+        logvars_out.reshape(1, comps, -1),
+    )
+
+
 def solution(mesh):
-    placed = (
-        P("grp", None, "blk", None),
-        P("grp", None),
-        P(None, "grp", None, "blk", None),
-        P("grp", None, "blk", None),
-        P(None, None, "blk"),
-        P(None, None, "blk"),
-        P(None, None, "blk"),
-        P(None, None, "blk"),
-        P(None, None, "blk"),
-        P(None, None, "blk"),
-        P(None, None, "blk"),
-        P(None, "blk"),
-        P(None, None, "blk"),
-        P(None, None, "blk"),
-    )
+    chips = mesh.shape["blk"]
+    if (mesh.shape["grp"], chips) == (2, HEADS):
+        mesh = Mesh(mesh.devices.reshape(2, chips // 4, 2, 2), EVERY)
+        blk, run = CHIPS, fast_device
+    else:
+        blk, run = "blk", per_device
+    cells = P("grp", None, blk, None)
+    columns = P(None, None, blk)
     return jax.shard_map(
-        per_device,
+        run,
         mesh=mesh,
-        in_specs=placed,
-        out_specs=(
-            P("grp", None, "blk", None),
-            P("grp", None, "blk", None),
-            P(),
-            P(None, None, "blk"),
-            P(None, None, "blk"),
-            P(None, None, "blk"),
-            P(None, None, "blk"),
-            P(None, None, "blk"),
-            P(None, None, "blk"),
-            P(None, None, "blk"),
-            P(None, "blk"),
-            P(None, None, "blk"),
-            P(None, None, "blk"),
-        ),
+        in_specs=(cells, P("grp", None), P(None, "grp", None, blk, None), cells)
+        + (columns,) * 7
+        + (P(None, blk), columns, columns),
+        out_specs=(cells, cells, P()) + (columns,) * 7 + (P(None, blk), columns, columns),
         check_vma=False,
     )

time: 2350 us -> 597 us (0.25)
  waiting for transfers between devices: 1620 us -> 220 us
  blocking collectives: 429 us -> 0 us
  starting transfers between devices: 1.41 us -> 134 us
  matrix products: 135 us -> 55.2 us
  local copies, waits for them, and re-layouts: 111 us -> 57.7 us
  Pallas kernels: 0 us -> 41.7 us
  other arithmetic: 24.9 us -> 62.7 us
    reduce_scatter x6 -> x0, waiting for transfers between devices: 1110 us -> none  [the longest x1 354 us: reduce_grads(): lax.psum_scatter(grad_back_w, 'blk', scatter_dimension=1, tiled=True)]
    all_gather x10 -> x0, waiting for transfers between devices: 385 us -> none  [the longest x1 134 us: gather_weights(): lax.all_gather(part_in, 'blk', axis=1, tiled=True)]
    all_gather x5 -> x0, blocking collectives: 228 us -> none  [the longest x1 53.2 us: layer_backward(): lax.all_gather(log_total, 'blk', axis=2, tiled=True)]
    ppermute x0 -> x76, waiting for transfers between devices: none -> 208 us  [the longest x65 200 us: hop(): return lax.ppermute(values, axis, [(i, i ^ step) for i in range(size)])]
    unnamed x2 -> x0, blocking collectives: 152 us -> none
    ppermute x0 -> x76, starting transfers between devices: none -> 112 us  [the longest x65 87 us: hop(): return lax.ppermute(values, axis, [(i, i ^ step) for i in range(size)])]
    unnamed x23 -> x0, waiting for transfers between devices: 109 us -> none
    dot_general x7 -> x0, matrix products: 56.8 us -> none  [the longest x1 10.8 us: layer_backward(): jnp.einsum('sqhd,skhd->shqk', grad_mixed_heads, heads_v, preferred_elemen...]
  transfers between devices with their start and end apart: 20 -> 80, of which waited for: 15 -> 23; matrix products, arithmetic and copies ran while one was open for 11% -> 28% of each run, Pallas kernels for 0% -> 7%
where the time goes in v1:
time: 597 us; the launch traced here: 589 us
  waiting for transfers between devices  220 us (37%)
  starting transfers between devices  134 us (22%)
  other arithmetic  62.7 us (11%)
  local copies, waits for them, and re-layouts  57.7 us (10%)
  matrix products  55.2 us (9%)
  Pallas kernels  41.7 us (7%)
  between operations  17.3 us (3%)
    ppermute x65, waiting for transfers between devices, hop(): return lax.ppermute(values, axis, [(i, i ^ step) for i in range(size)])  200 us
    ppermute x65, starting transfers between devices, hop(): return lax.ppermute(values, axis, [(i, i ^ step) for i in range(size)])  87 us
    pallas_call x6, Pallas kernels, copy_call(): pl.pallas_call(body, out_shape=out_shapes, in_specs=[anywhere] * len(oper...  28.2 us
    dot_general x10, matrix products, product(): return jnp.dot(left, right, preferred_element_type=jnp.float32)  21.4 us
    dot_general x9, matrix products, product_nt(): lax.dot_general(left, right, (((1,), (1,)), ((), ())), preferred_element_...  17.4 us
    dot_general x6, matrix products, product_tn(): lax.dot_general(left, right, (((0,), (0,)), ((), ())), preferred_element_...  16.3 us
    unnamed x203, local copies, waits for them, and re-layouts  14 us
    ppermute x5, starting transfers between devices, swap_groups(): return lax.ppermute(values, ('grp', 'x'), [(0, 0), (1, 2), (2, 1), (3, 3)])  12.6 us
  transfers between devices with their start and end apart: 80, of which 23 were waited for; matrix products, arithmetic and copies ran while one was open for 28% of the time, Pallas kernels for 7%

profile of v1, /device:TPU:0, one launch (start us, length us, event | category | flops | bytes accessed | tf_op | source)
XLA Modules:
  0.0 588.9 jit_solution(8806799748027689736)
XLA Ops:
  3.6 5.0 collective-permute-start.16
  8.7 3.4 collective-permute-start.11
  32.7 8.0 %collective-permute-done.11 = bf16[64,1024]{1,0:T(8,128)(2,1)S(1)} collective-permute-done((bf16[64,1024]{1,0:T(8,128)(2,1)S(1)}, bf16[64,1024]{1,0:T(8,128)(2,1)S(1)}, u32[]{:S(2)}, u32[]{:S(2)}) %collective-permute-start.11) | collective-permute-done | bytes 131104 | tf_op jit(solution)/shard_map/ppermute | solution.py:900
  40.7 7.3 %collective-permute-start.40 = (bf16[96,1024]{1,0:T(8,128)(2,1)}, bf16[96,1024]{1,0:T(8,128)(2,1)S(1)}, u32[]{:S(2)}, u32[]{:S(2)}) collective-permute-start(bf16[96,1024]{1,0:T(8,128)(2,1)} %get-tuple-element.231), channel_id=1, source_target_pairs={{0,8},{4,12},{8,0},{12,4},{1,9},{5,13},{9,1},{13,5},{2,10},{6,14},... | collective-permute-start | bytes 589832 | tf_op jit(solution)/shard_map/ppermute | solution.py:493
  48.0 6.4 %collective-permute-start.39 = (bf16[96,1024]{1,0:T(8,128)(2,1)}, bf16[96,1024]{1,0:T(8,128)(2,1)S(1)}, u32[]{:S(2)}, u32[]{:S(2)}) collective-permute-start(bf16[96,1024]{1,0:T(8,128)(2,1)} %get-tuple-element.231), channel_id=1, source_target_pairs={{0,4},{4,0},{8,12},{12,8},{1,5},{5,1},{9,13},{13,9},{2,6},{6,2},{1... | collective-permute-start | bytes 589832 | tf_op jit(solution)/shard_map/ppermute | solution.py:493
  55.5 3.9 collective-permute-start.14
  59.4 2.8 collective-permute-done.40
  63.4 5.2 collective-permute-start.25
  72.1 10.9 %collective-permute-start.3 = (bf16[144,1024]{1,0:T(8,128)(2,1)S(1)}, bf16[144,1024]{1,0:T(8,128)(2,1)S(1)}, u32[]{:S(2)}, u32[]{:S(2)}) collective-permute-start(bf16[144,1024]{1,0:T(8,128)(2,1)S(1)} %collective-permute-done), channel_id=1, source_target_pairs={{0,12},{4,8},{8,4},{12,0},{1,13},{5,9},{9,5},{13,1},{2,14},{6,10},... | collective-permute-start | bytes 884744 | tf_op jit(solution)/shard_map/ppermute | solution.py:493
  84.2 12.1 %collective-permute-start.2 = (bf16[144,1024]{1,0:T(8,128)(2,1)S(1)}, bf16[144,1024]{1,0:T(8,128)(2,1)S(1)}, u32[]{:S(2)}, u32[]{:S(2)}) collective-permute-start(bf16[144,1024]{1,0:T(8,128)(2,1)S(1)} %collective-permute-done), channel_id=1, source_target_pairs={{0,8},{4,12},{8,0},{12,4},{1,9},{5,13},{9,1},{13,5},{2,10},{6,14},... | collective-permute-start | bytes 884744 | tf_op jit(solution)/shard_map/ppermute | solution.py:493
  96.3 15.6 %collective-permute-done.24 = bf16[176,1024]{1,0:T(8,128)(2,1)S(1)} collective-permute-done((bf16[176,1024]{1,0:T(8,128)(2,1)S(1)}, bf16[176,1024]{1,0:T(8,128)(2,1)S(1)}, u32[]{:S(2)}, u32[]{:S(2)}) %collective-permute-start.24) | collective-permute-done | bytes 360480 | tf_op jit(solution)/shard_map/ppermute | solution.py:493
  115.7 8.8 %collective-permute-done.2 = bf16[144,1024]{1,0:T(8,128)(2,1)S(1)} collective-permute-done((bf16[144,1024]{1,0:T(8,128)(2,1)S(1)}, bf16[144,1024]{1,0:T(8,128)(2,1)S(1)}, u32[]{:S(2)}, u32[]{:S(2)}) %collective-permute-start.2) | collective-permute-done | bytes 294944 | tf_op jit(solution)/shard_map/ppermute | solution.py:493
  124.5 2.5 collective-permute-done.1
  130.5 5.7 collective-permute-done.6
  136.2 6.3 %collective-permute-done.5 = bf16[144,1024]{1,0:T(8,128)(2,1)S(1)} collective-permute-done((bf16[144,1024]{1,0:T(8,128)(2,1)S(1)}, bf16[144,1024]{1,0:T(8,128)(2,1)S(1)}, u32[]{:S(2)}, u32[]{:S(2)}) %collective-permute-start.5) | collective-permute-done | bytes 294944 | tf_op jit(solution)/shard_map/ppermute | solution.py:493
  147.0 9.5 %collective-permute-done.19 = bf16[4,160,512]{2,1,0:T(8,128)(2,1)S(1)} collective-permute-done((bf16[4,160,512]{2,1,0:T(8,128)(2,1)S(1)}, bf16[4,160,512]{2,1,0:T(8,128)(2,1)S(1)}, u32[]{:S(2)}, u32[]{:S(2)}) %collective-permute-start.19) | collective-permute-done | bytes 655392 | tf_op jit(solution)/shard_map/ppermute | solution.py:493
  157.7 2.0 collective-permute-start.20
  162.1 2.1 fusion.7
  164.5 2.8 fusion.151
  168.0 3.0 slice_bitcast_fusion.14
  171.1 12.5 %collective-permute-done.18.left_off = bf16[2,4,160,512]{3,2,1,0:T(8,128)(2,1)} collective-permute-done((bf16[2,4,160,512]{3,2,1,0:T(8,128)(2,1)}, bf16[2,4,160,512]{3,2,1,0:T(8,128)(2,1)}, u32[]{:S(2)}, u32[]{:S(2)}) %collective-permute-start.18) | collective-permute-done | bytes 1310752 | tf_op jit(solution)/shard_map/ppermute | solution.py:493
  183.5 6.2 %collective-permute-done.20.right_off = bf16[2,4,160,512]{3,2,1,0:T(8,128)(2,1)} collective-permute-done((bf16[2,4,160,512]{3,2,1,0:T(8,128)(2,1)}, bf16[2,4,160,512]{3,2,1,0:T(8,128)(2,1)}, u32[]{:S(2)}, u32[]{:S(2)}) %collective-permute-start.20) | collective-permute-done | bytes 1310752 | tf_op jit(solution)/shard_map/ppermute | solution.py:493
  189.8 5.5 shard_map.248
  196.4 3.6 collective-permute-start.35
  200.0 5.5 shard_map.247
  207.1 5.3 all-to-all-start
  213.6 2.0 collective-permute-start.44
  218.4 2.1 collective-permute-start.27
  220.5 2.4 pad_maximum_fusion.4.right_near
  226.2 1.9 fusion.150
  229.4 1.9 pad_maximum_fusion.17.right_near
  235.2 39.6 %collective-permute-done.27.left_off = bf16[2,4,176,512]{3,2,1,0:T(8,128)(2,1)} collective-permute-done((bf16[2,4,176,512]{3,2,1,0:T(8,128)(2,1)S(1)}, bf16[2,4,176,512]{3,2,1,0:T(8,128)(2,1)}, u32[]{:S(2)}, u32[]{:S(2)}) %collective-permute-start.27) | collective-permute-done | bytes 1441824 | tf_op jit(solution)/shard_map/ppermute | solution.py:493
  277.1 6.3 %shard_map.249 = (bf16[1024,2048]{1,0:T(8,128)(2,1)}, bf16[1024,512]{1,0:T(8,128)(2,1)}, bf16[1024,256]{1,0:T(8,128)(2,1)S(1)}) custom-call(bf16[2,4,176,512]{3,2,1,0:T(8,128)(2,1)S(1)} %pad_maximum_fusion.3.left_near, bf16[2,4,176,512]{3,2,1,0:T(8,128)(2,1)} %collective-permute-done.27.left_off, bf16[2,4,176,512]{3,2,1,0:T(8,128)(2,1)S(1)} %copy-done.2, ...), custom_call_target="tpu_custom_call" | custom-call | tf_op jit(solution)/shard_map/pallas_call | solution.py:564
  284.0 2.5 convolution_add_fusion
  297.9 5.0 shard_map.251
  306.5 2.0 fusion.130
  316.9 3.6 fusion.13
  326.3 1.9 fusion.93
  330.9 2.1 fusion.32
  337.8 5.5 collective-permute-start.34
  344.7 5.5 convert_reduce_fusion.1
  355.2 4.5 convolution_convert_fusion.refs_0_
  359.7 6.0 %shard_map.253 = (bf16[2,4,176,512]{3,2,1,0:T(8,128)(2,1)S(1)}, bf16[2,4,176,512]{3,2,1,0:T(8,128)(2,1)}, bf16[2,4,176,512]{3,2,1,0:T(8,128)(2,1)S(1)}, bf16[2,4,176,512]{3,2,1,0:T(8,128)(2,1)}) custom-call(bf16[1024,2048]{1,0:T(8,128)(2,1)} %convolution_convert_fusion.refs_0_, bf16[1024,512]{1,0:T(8,128)(2,1)S(1)} %convolution_convert_fusion.2.refs_1_, ...), custom_call_target="tpu_custom_call" | custom-call | tf_op jit(solution)/shard_map/pallas_call | solution.py:564
  376.6 5.2 all-to-all-start.1
  381.8 4.6 convolution_convert_fusion.1.refs_1_
  391.6 4.7 shard_map.252
  400.5 4.1 all-to-all-done.1
  404.6 8.0 %shard_map.250 = (bf16[8,2,64,128]{3,2,1,0:T(8,128)(2,1)S(1)}, f32[8,2,64,256]{3,2,1,0:T(8,128)S(1)}, f32[8,2,64,256]{3,2,1,0:T(8,128)S(1)}) custom-call(bf16[8,2,64,384]{3,2,1,0:T(8,128)(2,1)S(1)} %bitcast.319, bf16[8,2,64,256]{3,2,1,0:T(8,128)(2,1)S(1)} %copy-done.5, f32[2,1,1024]{2,1,0:T(1,128)S(1)} %compare_select_fusion.bias_ref, ...), custom_call_target="tpu_custom_call" | custom-call | tf_op jit(solution)/shard_map/pallas_call | solution.py:814
  421.5 5.1 all-to-all-start.2
  427.0 2.7 fusion.155
  432.2 3.9 collective-permute-done.58
  438.0 16.4 %collective-permute-done.69 = bf16[4,176,512]{2,1,0:T(8,128)(2,1)} collective-permute-done((bf16[4,176,512]{2,1,0:T(8,128)(2,1)}, bf16[4,176,512]{2,1,0:T(8,128)(2,1)}, u32[]{:S(2)}, u32[]{:S(2)}) %collective-permute-start.69) | collective-permute-done | bytes 720928 | tf_op jit(solution)/shard_map/ppermute | solution.py:493
  457.4 3.5 collective-permute-start.74
  462.0 8.7 %collective-permute-done.74 = bf16[176,1024]{1,0:T(8,128)(2,1)S(1)} collective-permute-done((bf16[176,1024]{1,0:T(8,128)(2,1)S(1)}, bf16[176,1024]{1,0:T(8,128)(2,1)S(1)}, u32[]{:S(2)}, u32[]{:S(2)}) %collective-permute-start.74) | collective-permute-done | bytes 360480 | tf_op jit(solution)/shard_map/ppermute | solution.py:493
  472.1 18.2 %collective-permute-done.73 = bf16[176,1024]{1,0:T(8,128)(2,1)S(1)} collective-permute-done((bf16[176,1024]{1,0:T(8,128)(2,1)S(1)}, bf16[176,1024]{1,0:T(8,128)(2,1)S(1)}, u32[]{:S(2)}, u32[]{:S(2)}) %collective-permute-start.73) | collective-permute-done | bytes 360480 | tf_op jit(solution)/shard_map/ppermute | solution.py:493
  492.8 14.0 %collective-permute-done.59 = bf16[4,160,512]{2,1,0:T(8,128)(2,1)S(1)} collective-permute-done((bf16[4,160,512]{2,1,0:T(8,128)(2,1)S(1)}, bf16[4,160,512]{2,1,0:T(8,128)(2,1)S(1)}, u32[]{:S(2)}, u32[]{:S(2)}) %collective-permute-start.59) | collective-permute-done | bytes 655392 | tf_op jit(solution)/shard_map/ppermute | solution.py:493
  508.2 6.1 %collective-permute-start.52 = (bf16[64,1024]{1,0:T(8,128)(2,1)S(1)}, bf16[64,1024]{1,0:T(8,128)(2,1)S(1)}, u32[]{:S(2)}, u32[]{:S(2)}) collective-permute-start(bf16[64,1024]{1,0:T(8,128)(2,1)S(1)} %get-tuple-element.209), channel_id=1, source_target_pairs={{2,0},{20,1},{8,2},{26,3},{14,4},{16,5},{4,6},{22,7},{10,8},{28,9}... | collective-permute-start | bytes 393224 | tf_op jit(solution)/shard_map/ppermute | solution.py:1061
  515.2 3.6 collective-permute-start.60
  519.0 8.0 %collective-permute-done.62 = bf16[160,1024]{1,0:T(8,128)(2,1)S(1)} collective-permute-done((bf16[160,1024]{1,0:T(8,128)(2,1)S(1)}, bf16[160,1024]{1,0:T(8,128)(2,1)S(1)}, u32[]{:S(2)}, u32[]{:S(2)}) %collective-permute-start.62) | collective-permute-done | bytes 327712 | tf_op jit(solution)/shard_map/ppermute | solution.py:493
  526.9 18.6 %collective-permute-done.61 = bf16[160,1024]{1,0:T(8,128)(2,1)S(1)} collective-permute-done((bf16[160,1024]{1,0:T(8,128)(2,1)S(1)}, bf16[160,1024]{1,0:T(8,128)(2,1)S(1)}, u32[]{:S(2)}, u32[]{:S(2)}) %collective-permute-start.61) | collective-permute-done | bytes 327712 | tf_op jit(solution)/shard_map/ppermute | solution.py:493
  553.9 2.5 fusion.69
  556.6 2.6 broadcast_select_fusion.1
  560.9 6.3 %all-to-all-start.3 = ((f32[16,16,128]{2,1,0:T(8,128)}), f32[16,16,128]{2,1,0:T(8,128)S(1)}, u32[]{:S(2)}, u32[]{:S(2)}) async-start(f32[16,16,128]{2,1,0:T(8,128)} %bitcast.162), calls=%async_computation.3 | async-start | bytes 262144 | tf_op jit(solution)/shard_map/all_to_all | solution.py:1101
  567.5 7.8 %all-to-all-done.3 = f32[16,16,128]{2,1,0:T(8,128)S(1)} async-done(((f32[16,16,128]{2,1,0:T(8,128)}), f32[16,16,128]{2,1,0:T(8,128)S(1)}, u32[]{:S(2)}, u32[]{:S(2)}) %all-to-all-start.3) | async-done | bytes 131104 | tf_op jit(solution)/shard_map/all_to_all | solution.py:1101
  (570 shorter events, 159.9 us)
Async XLA Ops:
  3.6 66.4 %collective-permute-start.16 = (bf16[160,1024]{1,0:T(8,128)(2,1)}, bf16[160,1024]{1,0:T(8,128)(2,1)S(1)}, u32[]{:S(2)}, u32[]{:S(2)}) collective-permute-start(bf16[160,1024]{1,0:T(8,128)(2,1)} %get-tuple-element.219), channel_id=1, source_target_pairs={{0,12},{4,8},{8,4},{12,0},{1,13},{5,9},{9,5},{13,1},{2,14},{6,10},... | collective-permute-start | bytes 983048 | tf_op jit(solution)/shard_map/ppermute | solution.py:493
  8.6 61.9 %collective-permute-start.15 = (bf16[160,1024]{1,0:T(8,128)(2,1)}, bf16[160,1024]{1,0:T(8,128)(2,1)}, u32[]{:S(2)}, u32[]{:S(2)}) collective-permute-start(bf16[160,1024]{1,0:T(8,128)(2,1)} %get-tuple-element.219), channel_id=1, source_target_pairs={{0,8},{4,12},{8,0},{12,4},{1,9},{5,13},{9,1},{13,5},{2,10},{6,14},... | collective-permute-start | bytes 983048 | tf_op jit(solution)/shard_map/ppermute | solution.py:493
  8.7 32.0 %collective-permute-start.11 = (bf16[64,1024]{1,0:T(8,128)(2,1)S(1)}, bf16[64,1024]{1,0:T(8,128)(2,1)S(1)}, u32[]{:S(2)}, u32[]{:S(2)}) collective-permute-start(bf16[64,1024]{1,0:T(8,128)(2,1)S(1)} %get-tuple-element.216), channel_id=1, source_target_pairs={{0,2},{1,20},{2,8},{3,26},{4,14},{5,16},{6,4},{7,22},{8,10},{9,28}... | collective-permute-start | bytes 393224 | tf_op jit(solution)/shard_map/ppermute | solution.py:900
  12.1 28.6 %collective-permute-start.10 = (bf16[64,1024]{1,0:T(8,128)(2,1)S(1)}, bf16[64,1024]{1,0:T(8,128)(2,1)S(1)}, u32[]{:S(2)}, u32[]{:S(2)}) collective-permute-start(bf16[64,1024]{1,0:T(8,128)(2,1)S(1)} %get-tuple-element.217), channel_id=1, source_target_pairs={{0,16},{1,4},{2,22},{3,10},{4,28},{5,0},{6,18},{7,6},{8,24},{9,12}... | collective-permute-start | bytes 393224 | tf_op jit(solution)/shard_map/ppermute | solution.py:900
  13.2 34.8 %collective-permute-start.9 = (bf16[64,1024]{1,0:T(8,128)(2,1)S(1)}, bf16[64,1024]{1,0:T(8,128)(2,1)}, u32[]{:S(2)}, u32[]{:S(2)}) collective-permute-start(bf16[64,1024]{1,0:T(8,128)(2,1)S(1)} %get-tuple-element.215), channel_id=1, source_target_pairs={{0,0},{1,18},{2,6},{3,24},{4,12},{5,30},{6,2},{7,20},{8,8},{9,26},... | collective-permute-start | bytes 393224 | tf_op jit(solution)/shard_map/ppermute | solution.py:900
  40.7 21.4 %collective-permute-start.40 = (bf16[96,1024]{1,0:T(8,128)(2,1)}, bf16[96,1024]{1,0:T(8,128)(2,1)S(1)}, u32[]{:S(2)}, u32[]{:S(2)}) collective-permute-start(bf16[96,1024]{1,0:T(8,128)(2,1)} %get-tuple-element.231), channel_id=1, source_target_pairs={{0,8},{4,12},{8,0},{12,4},{1,9},{5,13},{9,1},{13,5},{2,10},{6,14},... | collective-permute-start | bytes 589832 | tf_op jit(solution)/shard_map/ppermute | solution.py:493
  48.0 15.3 %collective-permute-start.39 = (bf16[96,1024]{1,0:T(8,128)(2,1)}, bf16[96,1024]{1,0:T(8,128)(2,1)S(1)}, u32[]{:S(2)}, u32[]{:S(2)}) collective-permute-start(bf16[96,1024]{1,0:T(8,128)(2,1)} %get-tuple-element.231), channel_id=1, source_target_pairs={{0,4},{4,0},{8,12},{12,8},{1,5},{5,1},{9,13},{13,9},{2,6},{6,2},{1... | collective-permute-start | bytes 589832 | tf_op jit(solution)/shard_map/ppermute | solution.py:493
  55.5 16.6 %collective-permute-start.14 = (bf16[160,1024]{1,0:T(8,128)(2,1)}, bf16[160,1024]{1,0:T(8,128)(2,1)S(1)}, u32[]{:S(2)}, u32[]{:S(2)}) collective-permute-start(bf16[160,1024]{1,0:T(8,128)(2,1)} %get-tuple-element.219), channel_id=1, source_target_pairs={{0,4},{4,0},{8,12},{12,8},{1,5},{5,1},{9,13},{13,9},{2,6},{6,2},{1... | collective-permute-start | bytes 983048 | tf_op jit(solution)/shard_map/ppermute | solution.py:493
  63.4 20.8 %collective-permute-start.25 = (bf16[176,1024]{1,0:T(8,128)(2,1)S(1)}, bf16[176,1024]{1,0:T(8,128)(2,1)S(1)}, u32[]{:S(2)}, u32[]{:S(2)}) collective-permute-start(bf16[176,1024]{1,0:T(8,128)(2,1)S(1)} %maximum_maximum_fusion), channel_id=1, source_target_pairs={{0,12},{4,8},{8,4},{12,0},{1,13},{5,9},{9,5},{13,1},{2,14},{6,10},... | collective-permute-start | bytes 1081352 | tf_op jit(solution)/shard_map/ppermute | solution.py:493
  69.8 42.1 %collective-permute-start.24 = (bf16[176,1024]{1,0:T(8,128)(2,1)S(1)}, bf16[176,1024]{1,0:T(8,128)(2,1)S(1)}, u32[]{:S(2)}, u32[]{:S(2)}) collective-permute-start(bf16[176,1024]{1,0:T(8,128)(2,1)S(1)} %maximum_maximum_fusion), channel_id=1, source_target_pairs={{0,8},{4,12},{8,0},{12,4},{1,9},{5,13},{9,1},{13,5},{2,10},{6,14},... | collective-permute-start | bytes 1081352 | tf_op jit(solution)/shard_map/ppermute | solution.py:493
  70.0 42.3 %collective-permute-start.23 = (bf16[176,1024]{1,0:T(8,128)(2,1)S(1)}, bf16[176,1024]{1,0:T(8,128)(2,1)S(1)}, u32[]{:S(2)}, u32[]{:S(2)}) collective-permute-start(bf16[176,1024]{1,0:T(8,128)(2,1)S(1)} %maximum_maximum_fusion), channel_id=1, source_target_pairs={{0,4},{4,0},{8,12},{12,8},{1,5},{5,1},{9,13},{13,9},{2,6},{6,2},{1... | collective-permute-start | bytes 1081352 | tf_op jit(solution)/shard_map/ppermute | solution.py:493
  70.6 43.1 %collective-permute-start.12 = (bf16[3,64,1024]{2,1,0:T(8,128)(2,1)S(1)}, bf16[3,64,1024]{2,1,0:T(8,128)(2,1)S(1)}, u32[]{:S(2)}, u32[]{:S(2)}) collective-permute-start(bf16[3,64,1024]{2,1,0:T(8,128)(2,1)S(1)} %pad_maximum_fusion.24), channel_id=1, source_target_pairs={{0,16},{16,0},{1,17},{17,1},{2,18},{18,2},{3,19},{19,3},{4,20},{20... | collective-permute-start | bytes 1179656 | tf_op jit(solution)/shard_map/ppermute | solution.py:493
  72.1 43.3 %collective-permute-start.3 = (bf16[144,1024]{1,0:T(8,128)(2,1)S(1)}, bf16[144,1024]{1,0:T(8,128)(2,1)S(1)}, u32[]{:S(2)}, u32[]{:S(2)}) collective-permute-start(bf16[144,1024]{1,0:T(8,128)(2,1)S(1)} %collective-permute-done), channel_id=1, source_target_pairs={{0,12},{4,8},{8,4},{12,0},{1,13},{5,9},{9,5},{13,1},{2,14},{6,10},... | collective-permute-start | bytes 884744 | tf_op jit(solution)/shard_map/ppermute | solution.py:493
  84.2 40.3 %collective-permute-start.2 = (bf16[144,1024]{1,0:T(8,128)(2,1)S(1)}, bf16[144,1024]{1,0:T(8,128)(2,1)S(1)}, u32[]{:S(2)}, u32[]{:S(2)}) collective-permute-start(bf16[144,1024]{1,0:T(8,128)(2,1)S(1)} %collective-permute-done), channel_id=1, source_target_pairs={{0,8},{4,12},{8,0},{12,4},{1,9},{5,13},{9,1},{13,5},{2,10},{6,14},... | collective-permute-start | bytes 884744 | tf_op jit(solution)/shard_map/ppermute | solution.py:493
  112.3 101.3 %collective-permute-start.42 = (bf16[4,96,512]{2,1,0:T(8,128)(2,1)}, bf16[4,96,512]{2,1,0:T(8,128)(2,1)}, u32[]{:S(2)}, u32[]{:S(2)}) collective-permute-start(bf16[4,96,512]{2,1,0:T(8,128)(2,1)} %get-tuple-element.180), channel_id=1, source_target_pairs={{0,1},{1,0},{2,3},{3,2},{4,5},{5,4},{6,7},{7,6},{8,9},{9,8},{10,11... | collective-permute-start | bytes 1179656 | tf_op jit(solution)/shard_map/ppermute | solution.py:493
  127.0 15.5 %collective-permute-start.5 = (bf16[144,1024]{1,0:T(8,128)(2,1)S(1)}, bf16[144,1024]{1,0:T(8,128)(2,1)S(1)}, u32[]{:S(2)}, u32[]{:S(2)}) collective-permute-start(bf16[144,1024]{1,0:T(8,128)(2,1)S(1)} %collective-permute-done.1), channel_id=1, source_target_pairs={{0,2},{2,0},{1,3},{3,1},{4,6},{6,4},{5,7},{7,5},{8,10},{10,8},{9,1... | collective-permute-start | bytes 884744 | tf_op jit(solution)/shard_map/ppermute | solution.py:493
  128.2 16.3 %collective-permute-start.17 = (bf16[4,160,512]{2,1,0:T(8,128)(2,1)S(1)}, bf16[4,160,512]{2,1,0:T(8,128)(2,1)S(1)}, u32[]{:S(2)}, u32[]{:S(2)}) collective-permute-start(bf16[4,160,512]{2,1,0:T(8,128)(2,1)S(1)} %get-tuple-element.168), channel_id=1, source_target_pairs={{0,1},{1,0},{2,3},{3,2},{4,5},{5,4},{6,7},{7,6},{8,9},{9,8},{10,11... | collective-permute-start | bytes 1966088 | tf_op jit(solution)/shard_map/ppermute | solution.py:493
  129.9 26.7 %collective-permute-start.19 = (bf16[4,160,512]{2,1,0:T(8,128)(2,1)S(1)}, bf16[4,160,512]{2,1,0:T(8,128)(2,1)S(1)}, u32[]{:S(2)}, u32[]{:S(2)}) collective-permute-start(bf16[4,160,512]{2,1,0:T(8,128)(2,1)S(1)} %get-tuple-element.167), channel_id=1, source_target_pairs={{0,2},{2,0},{1,3},{3,1},{4,6},{6,4},{5,7},{7,5},{8,10},{10,8},{9,1... | collective-permute-start | bytes 1966088 | tf_op jit(solution)/shard_map/ppermute | solution.py:493
  143.4 16.4 %collective-permute-start.8 = (bf16[8,16,1024]{2,1,0:T(8,128)(2,1)S(1)}, bf16[8,16,1024]{2,1,0:T(8,128)(2,1)S(1)}, u32[]{:S(2)}, u32[]{:S(2)}) collective-permute-start(bf16[8,16,1024]{2,1,0:T(8,128)(2,1)S(1)} %get-tuple-element.35), channel_id=1, source_target_pairs={{0,16},{16,0},{1,17},{17,1},{2,18},{18,2},{3,19},{19,3},{4,20},{20... | collective-permute-start | bytes 786440 | tf_op jit(solution)/shard_map/ppermute | solution.py:493
  145.8 37.7 %collective-permute-start.18 = (bf16[2,4,160,512]{3,2,1,0:T(8,128)(2,1)}, bf16[2,4,160,512]{3,2,1,0:T(8,128)(2,1)}, u32[]{:S(2)}, u32[]{:S(2)}) collective-permute-start(bf16[2,4,160,512]{3,2,1,0:T(8,128)(2,1)} %pad_maximum_fusion.6.left_near), channel_id=1, source_target_pairs={{0,2},{2,0},{1,3},{3,1},{4,6},{6,4},{5,7},{7,5},{8,10},{10,8},{9,1... | collective-permute-start | bytes 3932168 | tf_op jit(solution)/shard_map/ppermute | solution.py:493
  157.7 32.1 %collective-permute-start.20 = (bf16[2,4,160,512]{3,2,1,0:T(8,128)(2,1)}, bf16[2,4,160,512]{3,2,1,0:T(8,128)(2,1)}, u32[]{:S(2)}, u32[]{:S(2)}) collective-permute-start(bf16[2,4,160,512]{3,2,1,0:T(8,128)(2,1)} %pad_maximum_fusion.7.right_near), channel_id=1, source_target_pairs={{0,1},{1,0},{2,3},{3,2},{4,5},{5,4},{6,7},{7,6},{8,9},{9,8},{10,11... | collective-permute-start | bytes 3932168 | tf_op jit(solution)/shard_map/ppermute | solution.py:493
  167.9 28.4 %collective-permute-start.13 = (bf16[8,2,64,256]{3,2,1,0:T(8,128)(2,1)S(1)}, bf16[8,2,64,256]{3,2,1,0:T(8,128)(2,1)S(1)}, u32[]{:S(2)}, u32[]{:S(2)}) collective-permute-start(bf16[8,2,64,256]{3,2,1,0:T(8,128)(2,1)S(1)} %slice.465), channel_id=1, source_target_pairs={{0,16},{16,0},{1,17},{17,1},{2,18},{18,2},{3,19},{19,3},{4,20},{20... | collective-permute-start | bytes 1572872 | tf_op jit(solution)/shard_map/ppermute | solution.py:493
  171.0 45.7 %collective-permute-start.26 = (bf16[4,176,512]{2,1,0:T(8,128)(2,1)}, bf16[4,176,512]{2,1,0:T(8,128)(2,1)}, u32[]{:S(2)}, u32[]{:S(2)}) collective-permute-start(bf16[4,176,512]{2,1,0:T(8,128)(2,1)} %get-tuple-element.159), channel_id=1, source_target_pairs={{0,1},{1,0},{2,3},{3,2},{4,5},{5,4},{6,7},{7,6},{8,9},{9,8},{10,11... | collective-permute-start | bytes 2162696 | tf_op jit(solution)/shard_map/ppermute | solution.py:493
  195.3 28.9 %collective-permute-start.21 = (bf16[1024,512]{1,0:T(8,128)(2,1)}, bf16[1024,512]{1,0:T(8,128)(2,1)}, u32[]{:S(2)}, u32[]{:S(2)}) collective-permute-start(bf16[1024,512]{1,0:T(8,128)(2,1)} %get-tuple-element.37), channel_id=1, source_target_pairs={{0,16},{16,0},{1,17},{17,1},{2,18},{18,2},{3,19},{19,3},{4,20},{20... | collective-permute-start | bytes 3145736 | tf_op jit(solution)/shard_map/ppermute | solution.py:493
  195.5 22.8 %collective-permute-start.28 = (bf16[4,176,512]{2,1,0:T(8,128)(2,1)}, bf16[4,176,512]{2,1,0:T(8,128)(2,1)}, u32[]{:S(2)}, u32[]{:S(2)}) collective-permute-start(bf16[4,176,512]{2,1,0:T(8,128)(2,1)} %get-tuple-element.158), channel_id=1, source_target_pairs={{0,2},{2,0},{1,3},{3,1},{4,6},{6,4},{5,7},{7,5},{8,10},{10,8},{9,1... | collective-permute-start | bytes 2162696 | tf_op jit(solution)/shard_map/ppermute | solution.py:493
  196.4 93.5 %collective-permute-start.35 = (bf16[128,1024]{1,0:T(8,128)(2,1)}, bf16[128,1024]{1,0:T(8,128)(2,1)}, u32[]{:S(2)}, u32[]{:S(2)}) collective-permute-start(bf16[128,1024]{1,0:T(8,128)(2,1)} %bitcast.67), channel_id=1, source_target_pairs={{0,0},{1,16},{16,1},{17,17},{2,2},{3,18},{18,3},{19,19},{4,4},{5,2... | collective-permute-start | bytes 786440 | tf_op jit(solution)/shard_map/ppermute | solution.py:501
  207.1 17.3 %all-to-all-start = ((bf16[8,128,128]{1,2,0:T(8,128)(2,1)}), bf16[8,128,128]{1,2,0:T(8,128)(2,1)}, u32[]{:S(2)}, u32[]{:S(2)}) async-start(bf16[8,128,128]{1,2,0:T(8,128)(2,1)} %copy.90), calls=%async_computation | async-start | bytes 524288 | tf_op jit(solution)/shard_map/all_to_all | solution.py:958
  213.6 15.7 %collective-permute-start.44 = (bf16[4,96,512]{2,1,0:T(8,128)(2,1)}, bf16[4,96,512]{2,1,0:T(8,128)(2,1)}, u32[]{:S(2)}, u32[]{:S(2)}) collective-permute-start(bf16[4,96,512]{2,1,0:T(8,128)(2,1)} %get-tuple-element.179), channel_id=1, source_target_pairs={{0,2},{2,0},{1,3},{3,1},{4,6},{6,4},{5,7},{7,5},{8,10},{10,8},{9,1... | collective-permute-start | bytes 1179656 | tf_op jit(solution)/shard_map/ppermute | solution.py:493
  216.8 77.9 %collective-permute-start.43 = (bf16[2,4,96,512]{3,2,1,0:T(8,128)(2,1)S(1)}, bf16[2,4,96,512]{3,2,1,0:T(8,128)(2,1)}, u32[]{:S(2)}, u32[]{:S(2)}) collective-permute-start(bf16[2,4,96,512]{3,2,1,0:T(8,128)(2,1)S(1)} %pad_maximum_fusion.16.left_near), channel_id=1, source_target_pairs={{0,2},{2,0},{1,3},{3,1},{4,6},{6,4},{5,7},{7,5},{8,10},{10,8},{9,1... | collective-permute-start | bytes 2359304 | tf_op jit(solution)/shard_map/ppermute | solution.py:493
  218.4 56.4 %collective-permute-start.27 = (bf16[2,4,176,512]{3,2,1,0:T(8,128)(2,1)S(1)}, bf16[2,4,176,512]{3,2,1,0:T(8,128)(2,1)}, u32[]{:S(2)}, u32[]{:S(2)}) collective-permute-start(bf16[2,4,176,512]{3,2,1,0:T(8,128)(2,1)S(1)} %pad_maximum_fusion.3.left_near), channel_id=1, source_target_pairs={{0,2},{2,0},{1,3},{3,1},{4,6},{6,4},{5,7},{7,5},{8,10},{10,8},{9,1... | collective-permute-start | bytes 4325384 | tf_op jit(solution)/shard_map/ppermute | solution.py:493
  224.2 51.5 %collective-permute-start.29 = (bf16[2,4,176,512]{3,2,1,0:T(8,128)(2,1)}, bf16[2,4,176,512]{3,2,1,0:T(8,128)(2,1)}, u32[]{:S(2)}, u32[]{:S(2)}) collective-permute-start(bf16[2,4,176,512]{3,2,1,0:T(8,128)(2,1)} %pad_maximum_fusion.4.right_near), channel_id=1, source_target_pairs={{0,1},{1,0},{2,3},{3,2},{4,5},{5,4},{6,7},{7,6},{8,9},{9,8},{10,11... | collective-permute-start | bytes 4325384 | tf_op jit(solution)/shard_map/ppermute | solution.py:493
  229.3 54.2 %collective-permute-start.22 = (bf16[128,1024]{1,0:T(8,128)(2,1)}, bf16[128,1024]{1,0:T(8,128)(2,1)}, u32[]{:S(2)}, u32[]{:S(2)}) collective-permute-start(bf16[128,1024]{1,0:T(8,128)(2,1)} %add_convert_fusion.3), channel_id=1, source_target_pairs={{0,16},{16,0},{1,17},{17,1},{2,18},{18,2},{3,19},{19,3},{4,20},{20... | collective-permute-start | bytes 786440 | tf_op jit(solution)/shard_map/ppermute | solution.py:493
  274.8 21.5 %collective-permute-start.45 = (bf16[2,4,96,512]{3,2,1,0:T(8,128)(2,1)}, bf16[2,4,96,512]{3,2,1,0:T(8,128)(2,1)}, u32[]{:S(2)}, u32[]{:S(2)}) collective-permute-start(bf16[2,4,96,512]{3,2,1,0:T(8,128)(2,1)} %pad_maximum_fusion.17.right_near), channel_id=1, source_target_pairs={{0,1},{1,0},{2,3},{3,2},{4,5},{5,4},{6,7},{7,6},{8,9},{9,8},{10,11... | collective-permute-start | bytes 2359304 | tf_op jit(solution)/shard_map/ppermute | solution.py:493
  283.4 19.6 %collective-permute-start.33 = (bf16[1024,256]{1,0:T(8,128)(2,1)S(1)}, bf16[1024,256]{1,0:T(8,128)(2,1)}, u32[]{:S(2)}, u32[]{:S(2)}) collective-permute-start(bf16[1024,256]{1,0:T(8,128)(2,1)S(1)} %get-tuple-element.41), channel_id=1, source_target_pairs={{0,16},{16,0},{1,17},{17,1},{2,18},{18,2},{3,19},{19,3},{4,20},{20... | collective-permute-start | bytes 1572872 | tf_op jit(solution)/shard_map/ppermute | solution.py:493
  283.5 25.0 %collective-permute-start.31 = (bf16[1024,512]{1,0:T(8,128)(2,1)}, bf16[1024,512]{1,0:T(8,128)(2,1)}, u32[]{:S(2)}, u32[]{:S(2)}) collective-permute-start(bf16[1024,512]{1,0:T(8,128)(2,1)} %get-tuple-element.40), channel_id=1, source_target_pairs={{0,16},{16,0},{1,17},{17,1},{2,18},{18,2},{3,19},{19,3},{4,20},{20... | collective-permute-start | bytes 3145736 | tf_op jit(solution)/shard_map/ppermute | solution.py:493
  289.9 16.5 %collective-permute-start.30 = (f32[128,1024]{1,0:T(8,128)}, f32[128,1024]{1,0:T(8,128)}, u32[]{:S(2)}, u32[]{:S(2)}) collective-permute-start(f32[128,1024]{1,0:T(8,128)} %slice.487), channel_id=1, source_target_pairs={{0,16},{16,0},{1,17},{17,1},{2,18},{18,2},{3,19},{19,3},{4,20},{20... | collective-permute-start | bytes 1572872 | tf_op jit(solution)/shard_map/ppermute | solution.py:493
  294.7 17.2 %collective-permute-start.32 = (f32[128,512]{1,0:T(8,128)}, f32[128,512]{1,0:T(8,128)S(1)}, u32[]{:S(2)}, u32[]{:S(2)}) collective-permute-start(f32[128,512]{1,0:T(8,128)} %bitcast.382), channel_id=1, source_target_pairs={{0,0},{1,16},{16,1},{17,17},{2,2},{3,18},{18,3},{19,19},{4,4},{5,2... | collective-permute-start | bytes 786440 | tf_op jit(solution)/shard_map/ppermute | solution.py:501
  296.3 41.1 %collective-permute-start.66 = (bf16[128,1024]{1,0:T(8,128)(2,1)}, bf16[128,1024]{1,0:T(8,128)(2,1)}, u32[]{:S(2)}, u32[]{:S(2)}) collective-permute-start(bf16[128,1024]{1,0:T(8,128)(2,1)} %collective-permute-done.35), channel_id=1, source_target_pairs={{0,16},{16,0},{1,17},{17,1},{2,18},{18,2},{3,19},{19,3},{4,20},{20... | collective-permute-start | bytes 786440 | tf_op jit(solution)/shard_map/ppermute | solution.py:493
  302.9 87.1 %collective-permute-start.55 = (bf16[128,1024]{0,1:T(8,128)(2,1)}, bf16[128,1024]{0,1:T(8,128)(2,1)}, u32[]{:S(2)}, u32[]{:S(2)}) collective-permute-start(bf16[128,1024]{0,1:T(8,128)(2,1)} %bitcast.34), channel_id=1, source_target_pairs={{0,16},{16,0},{1,17},{17,1},{2,18},{18,2},{3,19},{19,3},{4,20},{20... | collective-permute-start | bytes 786440 | tf_op jit(solution)/shard_map/ppermute | solution.py:493
  322.9 30.5 %collective-permute-start.64 = (bf16[128,1024]{1,0:T(8,128)(2,1)S(1)}, bf16[128,1024]{1,0:T(8,128)(2,1)}, u32[]{:S(2)}, u32[]{:S(2)}) collective-permute-start(bf16[128,1024]{1,0:T(8,128)(2,1)S(1)} %get-tuple-element.137), channel_id=1, source_target_pairs={{0,16},{16,0},{1,17},{17,1},{2,18},{18,2},{3,19},{19,3},{4,20},{20... | collective-permute-start | bytes 786440 | tf_op jit(solution)/shard_map/ppermute | solution.py:493
  328.2 16.5 %collective-permute-start.36 = (bf16[128,1024]{1,0:T(8,128)(2,1)}, bf16[128,1024]{1,0:T(8,128)(2,1)}, u32[]{:S(2)}, u32[]{:S(2)}) collective-permute-start(bf16[128,1024]{1,0:T(8,128)(2,1)} %fusion.93), channel_id=1, source_target_pairs={{0,16},{16,0},{1,17},{17,1},{2,18},{18,2},{3,19},{19,3},{4,20},{20... | collective-permute-start | bytes 786440 | tf_op jit(solution)/shard_map/ppermute | solution.py:493
  337.5 16.0 %collective-permute-start.65 = (bf16[128,1024]{1,0:T(8,128)(2,1)S(1)}, bf16[128,1024]{1,0:T(8,128)(2,1)}, u32[]{:S(2)}, u32[]{:S(2)}) collective-permute-start(bf16[128,1024]{1,0:T(8,128)(2,1)S(1)} %get-tuple-element.149), channel_id=1, source_target_pairs={{0,16},{16,0},{1,17},{17,1},{2,18},{18,2},{3,19},{19,3},{4,20},{20... | collective-permute-start | bytes 786440 | tf_op jit(solution)/shard_map/ppermute | solution.py:493
  337.8 48.7 %collective-permute-start.34 = (f32[128,1024]{1,0:T(8,128)}, f32[128,1024]{1,0:T(8,128)}, u32[]{:S(2)}, u32[]{:S(2)}) collective-permute-start(f32[128,1024]{1,0:T(8,128)} %fusion.32), channel_id=1, source_target_pairs={{0,0},{1,16},{16,1},{17,17},{2,2},{3,18},{18,3},{19,19},{4,4},{5,2... | collective-permute-start | bytes 1572872 | tf_op jit(solution)/shard_map/ppermute | solution.py:501
  352.7 15.9 %collective-permute-start.37 = (f32[128,1024]{1,0:T(8,128)}, f32[128,1024]{1,0:T(8,128)}, u32[]{:S(2)}, u32[]{:S(2)}) collective-permute-start(f32[128,1024]{1,0:T(8,128)} %slice.496), channel_id=1, source_target_pairs={{0,16},{16,0},{1,17},{17,1},{2,18},{18,2},{3,19},{19,3},{4,20},{20... | collective-permute-start | bytes 1572872 | tf_op jit(solution)/shard_map/ppermute | solution.py:493
  365.7 47.0 %collective-permute-start.68 = (bf16[2,4,176,512]{3,2,1,0:T(8,128)(2,1)}, bf16[2,4,176,512]{3,2,1,0:T(8,128)(2,1)}, u32[]{:S(2)}, u32[]{:S(2)}) collective-permute-start(bf16[2,4,176,512]{3,2,1,0:T(8,128)(2,1)} %get-tuple-element.52), channel_id=1, source_target_pairs={{0,1},{1,0},{2,3},{3,2},{4,5},{5,4},{6,7},{7,6},{8,9},{9,8},{10,11... | collective-permute-start | bytes 4325384 | tf_op jit(solution)/shard_map/ppermute | solution.py:493
  367.1 48.5 %collective-permute-start.70 = (bf16[2,4,176,512]{3,2,1,0:T(8,128)(2,1)}, bf16[2,4,176,512]{3,2,1,0:T(8,128)(2,1)}, u32[]{:S(2)}, u32[]{:S(2)}) collective-permute-start(bf16[2,4,176,512]{3,2,1,0:T(8,128)(2,1)} %get-tuple-element.54), channel_id=1, source_target_pairs={{0,2},{2,0},{1,3},{3,1},{4,6},{6,4},{5,7},{7,5},{8,10},{10,8},{9,1... | collective-permute-start | bytes 4325384 | tf_op jit(solution)/shard_map/ppermute | solution.py:493
  372.6 17.5 %collective-permute-start.54 = (bf16[128,1024]{1,0:T(8,128)(2,1)S(1)}, bf16[128,1024]{1,0:T(8,128)(2,1)}, u32[]{:S(2)}, u32[]{:S(2)}) collective-permute-start(bf16[128,1024]{1,0:T(8,128)(2,1)S(1)} %convert_element_type.211), channel_id=1, source_target_pairs={{0,16},{16,0},{1,17},{17,1},{2,18},{18,2},{3,19},{19,3},{4,20},{20... | collective-permute-start | bytes 786440 | tf_op jit(solution)/shard_map/ppermute | solution.py:493
  376.6 28.0 %all-to-all-start.1 = ((bf16[8,128,128]{2,1,0:T(8,128)(2,1)}), bf16[8,128,128]{2,1,0:T(8,128)(2,1)S(1)}, u32[]{:S(2)}, u32[]{:S(2)}) async-start(bf16[8,128,128]{2,1,0:T(8,128)(2,1)} %maximum_bitcast_fusion.1), calls=%async_computation.1 | async-start | bytes 524288 | tf_op jit(solution)/shard_map/all_to_all | solution.py:1005
  386.5 167.4 %collective-permute-start.46 = (bf16[3072,512]{1,0:T(8,128)(2,1)}, bf16[3072,512]{1,0:T(8,128)(2,1)}, u32[]{:S(2)}, u32[]{:S(2)}) collective-permute-start(bf16[3072,512]{1,0:T(8,128)(2,1)} %shard_map.251), channel_id=1, source_target_pairs={{0,16},{16,0},{1,17},{17,1},{2,18},{18,2},{3,19},{19,3},{4,20},{20... | collective-permute-start | bytes 9437192 | tf_op jit(solution)/shard_map/ppermute | solution.py:493
  398.5 31.9 %collective-permute-start.56 = (bf16[2,4,160,512]{3,2,1,0:T(8,128)(2,1)}, bf16[2,4,160,512]{3,2,1,0:T(8,128)(2,1)}, u32[]{:S(2)}, u32[]{:S(2)}) collective-permute-start(bf16[2,4,160,512]{3,2,1,0:T(8,128)(2,1)} %get-tuple-element.48), channel_id=1, source_target_pairs={{0,1},{1,0},{2,3},{3,2},{4,5},{5,4},{6,7},{7,6},{8,9},{9,8},{10,11... | collective-permute-start | bytes 3932168 | tf_op jit(solution)/shard_map/ppermute | solution.py:493
  398.6 37.5 %collective-permute-start.58 = (bf16[2,4,160,512]{3,2,1,0:T(8,128)(2,1)}, bf16[2,4,160,512]{3,2,1,0:T(8,128)(2,1)}, u32[]{:S(2)}, u32[]{:S(2)}) collective-permute-start(bf16[2,4,160,512]{3,2,1,0:T(8,128)(2,1)} %get-tuple-element.50), channel_id=1, source_target_pairs={{0,2},{2,0},{1,3},{3,1},{4,6},{6,4},{5,7},{7,5},{8,10},{10,8},{9,1... | collective-permute-start | bytes 3932168 | tf_op jit(solution)/shard_map/ppermute | solution.py:493
  415.6 38.7 %collective-permute-start.69 = (bf16[4,176,512]{2,1,0:T(8,128)(2,1)}, bf16[4,176,512]{2,1,0:T(8,128)(2,1)}, u32[]{:S(2)}, u32[]{:S(2)}) collective-permute-start(bf16[4,176,512]{2,1,0:T(8,128)(2,1)} %fusion.37), channel_id=1, source_target_pairs={{0,2},{2,0},{1,3},{3,1},{4,6},{6,4},{5,7},{7,5},{8,10},{10,8},{9,1... | collective-permute-start | bytes 2162696 | tf_op jit(solution)/shard_map/ppermute | solution.py:493
  419.7 36.0 %collective-permute-start.71 = (bf16[4,176,512]{2,1,0:T(8,128)(2,1)}, bf16[4,176,512]{2,1,0:T(8,128)(2,1)}, u32[]{:S(2)}, u32[]{:S(2)}) collective-permute-start(bf16[4,176,512]{2,1,0:T(8,128)(2,1)} %fusion.38), channel_id=1, source_target_pairs={{0,1},{1,0},{2,3},{3,2},{4,5},{5,4},{6,7},{7,6},{8,9},{9,8},{10,11... | collective-permute-start | bytes 2162696 | tf_op jit(solution)/shard_map/ppermute | solution.py:493
  421.5 132.1 %all-to-all-start.2 = ((bf16[8,128,384]{1,2,0:T(8,128)(2,1)}), bf16[8,128,384]{1,2,0:T(8,128)(2,1)S(1)}, u32[]{:S(2)}, u32[]{:S(2)}) async-start(bf16[8,128,384]{1,2,0:T(8,128)(2,1)} %copy.104), calls=%async_computation.2 | async-start | bytes 1572864 | tf_op jit(solution)/shard_map/all_to_all | solution.py:1043
  430.5 76.8 %collective-permute-start.49 = (f32[3,1,64,1024]{3,2,1,0:T(8,128)S(1)}, f32[3,1,64,1024]{3,2,1,0:T(8,128)S(1)}, u32[]{:S(2)}, u32[]{:S(2)}) collective-permute-start(f32[3,1,64,1024]{3,2,1,0:T(8,128)S(1)} %constant_dynamic-slice_fusion), channel_id=1, source_target_pairs={{0,16},{16,0},{1,17},{17,1},{2,18},{18,2},{3,19},{19,3},{4,20},{20... | collective-permute-start | bytes 2359304 | tf_op jit(solution)/shard_map/ppermute | solution.py:493
  460.9 29.4 %collective-permute-start.73 = (bf16[176,1024]{1,0:T(8,128)(2,1)S(1)}, bf16[176,1024]{1,0:T(8,128)(2,1)S(1)}, u32[]{:S(2)}, u32[]{:S(2)}) collective-permute-start(bf16[176,1024]{1,0:T(8,128)(2,1)S(1)} %get-tuple-element.155), channel_id=1, source_target_pairs={{0,8},{4,12},{8,0},{12,4},{1,9},{5,13},{9,1},{13,5},{2,10},{6,14},... | collective-permute-start | bytes 1081352 | tf_op jit(solution)/shard_map/ppermute | solution.py:493
  461.1 30.5 %collective-permute-start.72 = (bf16[176,1024]{1,0:T(8,128)(2,1)S(1)}, bf16[176,1024]{1,0:T(8,128)(2,1)S(1)}, u32[]{:S(2)}, u32[]{:S(2)}) collective-permute-start(bf16[176,1024]{1,0:T(8,128)(2,1)S(1)} %get-tuple-element.153), channel_id=1, source_target_pairs={{0,4},{4,0},{8,12},{12,8},{1,5},{5,1},{9,13},{13,9},{2,6},{6,2},{1... | collective-permute-start | bytes 1081352 | tf_op jit(solution)/shard_map/ppermute | solution.py:493
  470.7 21.8 %collective-permute-start.57 = (bf16[4,160,512]{2,1,0:T(8,128)(2,1)S(1)}, bf16[4,160,512]{2,1,0:T(8,128)(2,1)S(1)}, u32[]{:S(2)}, u32[]{:S(2)}) collective-permute-start(bf16[4,160,512]{2,1,0:T(8,128)(2,1)S(1)} %fusion.44), channel_id=1, source_target_pairs={{0,2},{2,0},{1,3},{3,1},{4,6},{6,4},{5,7},{7,5},{8,10},{10,8},{9,1... | collective-permute-start | bytes 1966088 | tf_op jit(solution)/shard_map/ppermute | solution.py:493
  490.3 16.5 %collective-permute-start.59 = (bf16[4,160,512]{2,1,0:T(8,128)(2,1)S(1)}, bf16[4,160,512]{2,1,0:T(8,128)(2,1)S(1)}, u32[]{:S(2)}, u32[]{:S(2)}) collective-permute-start(bf16[4,160,512]{2,1,0:T(8,128)(2,1)S(1)} %fusion.45), channel_id=1, source_target_pairs={{0,1},{1,0},{2,3},{3,2},{4,5},{5,4},{6,7},{7,6},{8,9},{9,8},{10,11... | collective-permute-start | bytes 1966088 | tf_op jit(solution)/shard_map/ppermute | solution.py:493
  514.4 31.1 %collective-permute-start.61 = (bf16[160,1024]{1,0:T(8,128)(2,1)S(1)}, bf16[160,1024]{1,0:T(8,128)(2,1)S(1)}, u32[]{:S(2)}, u32[]{:S(2)}) collective-permute-start(bf16[160,1024]{1,0:T(8,128)(2,1)S(1)} %get-tuple-element.164), channel_id=1, source_target_pairs={{0,8},{4,12},{8,0},{12,4},{1,9},{5,13},{9,1},{13,5},{2,10},{6,14},... | collective-permute-start | bytes 983048 | tf_op jit(solution)/shard_map/ppermute | solution.py:493
  515.2 30.4 %collective-permute-start.60 = (bf16[160,1024]{1,0:T(8,128)(2,1)S(1)}, bf16[160,1024]{1,0:T(8,128)(2,1)S(1)}, u32[]{:S(2)}, u32[]{:S(2)}) collective-permute-start(bf16[160,1024]{1,0:T(8,128)(2,1)S(1)} %get-tuple-element.162), channel_id=1, source_target_pairs={{0,4},{4,0},{8,12},{12,8},{1,5},{5,1},{9,13},{13,9},{2,6},{6,2},{1... | collective-permute-start | bytes 983048 | tf_op jit(solution)/shard_map/ppermute | solution.py:493
  518.8 29.3 %collective-permute-start.75 = (f32[176,1024]{1,0:T(8,128)S(1)}, f32[176,1024]{1,0:T(8,128)S(1)}, u32[]{:S(2)}, u32[]{:S(2)}) collective-permute-start(f32[176,1024]{1,0:T(8,128)S(1)} %fusion.43), channel_id=1, source_target_pairs={{0,16},{16,0},{1,17},{17,1},{2,18},{18,2},{3,19},{19,3},{4,20},{20... | collective-permute-start | bytes 2162696 | tf_op jit(solution)/shard_map/ppermute | solution.py:493
  526.9 25.7 %collective-permute-start.53 = (bf16[192,1024]{1,0:T(8,128)(2,1)S(1)}, bf16[192,1024]{1,0:T(8,128)(2,1)S(1)}, u32[]{:S(2)}, u32[]{:S(2)}) collective-permute-start(bf16[192,1024]{1,0:T(8,128)(2,1)S(1)} %constant_dynamic-update-slice_fusion), channel_id=1, source_target_pairs={{0,16},{16,0},{1,17},{17,1},{2,18},{18,2},{3,19},{19,3},{4,20},{20... | collective-permute-start | bytes 1179656 | tf_op jit(solution)/shard_map/ppermute | solution.py:493
  546.6 33.9 %collective-permute-start.63 = (f32[160,1024]{1,0:T(8,128)}, f32[160,1024]{1,0:T(8,128)}, u32[]{:S(2)}, u32[]{:S(2)}) collective-permute-start(f32[160,1024]{1,0:T(8,128)} %fusion.50), channel_id=1, source_target_pairs={{0,16},{16,0},{1,17},{17,1},{2,18},{18,2},{3,19},{19,3},{4,20},{20... | collective-permute-start | bytes 1966088 | tf_op jit(solution)/shard_map/ppermute | solution.py:493
  (114 other events, 918.6 us)
